TPU v7x, 32 devices: a whole 2x2x4 slice. The times are simulated.
32 devices in a mesh: section: 4 (over y, x), batch: 8 (over z, core).
Axes of the slice: x: 2, y: 2, z: 4, core: 2. Of those that a mesh axis runs over, the one named last changes fastest.
Arguments:
- latents: bfloat16 [8192, 1024], P('batch'), may hold values from -400 to 400
- points: bfloat16 [4096, 1024], P('batch'), may hold values from -6 to 6
- neighbours: int32 [32, 256], P('batch'), may hold values from 0 to 511
- lengths: int32 [32], P('batch'), may hold values from 64 to 256, as said below
- cross_proj: bfloat16 [1024, 3, 1024], P('batch'), may hold values from -0.1875 to 0.1875
- cross_out: bfloat16 [1024, 1024], P('batch'), may hold values from -0.75 to 0.75
- cross_gains: bfloat16 [2, 1024], P(None, 'batch'), may hold values from 0.099609375 to 1.8984375
- self_proj: bfloat16 [1024, 3, 1024], P('batch'), may hold values from -0.1875 to 0.1875
- self_out: bfloat16 [1024, 1024], P('batch'), may hold values from -0.75 to 0.75
- self_gain: bfloat16 [1024], P('batch'), may hold values from 0.099609375 to 1.8984375
- mlp_gain: bfloat16 [2, 1024], P(None, 'batch'), may hold values from 0.099609375 to 1.8984375
- mlp_in: bfloat16 [2, 1024, 4096], P(None, 'batch'), may hold values from -0.1875 to 0.1875
- mlp_in_bias: bfloat16 [2, 4096], P(None, 'batch'), may hold values from -3 to 3
- mlp_down: bfloat16 [2, 1024, 4096], P(None, 'batch'), may hold values from -0.1875 to 0.1875
- mlp_out_bias: bfloat16 [2, 1024], P(None, 'batch'), may hold values from -2 to 2
- cotangent: bfloat16 [8192, 1024], P('batch'), may hold values from -6 to 6
Outputs:
- latents_out: bfloat16 [8192, 1024], P('batch')
- latents_grad: float32 [8192, 1024], P('batch')
- points_grad: float32 [4096, 1024], P('batch')
- cross_proj_grad: float32 [1024, 3, 1024], P('batch')
- cross_out_grad: float32 [1024, 1024], P('batch')
- cross_gains_grad: float32 [2, 1024], P(None, 'batch')
- self_proj_grad: float32 [1024, 3, 1024], P('batch')
- self_out_grad: float32 [1024, 1024], P('batch')
- self_gain_grad: float32 [1024], P('batch')
- mlp_gain_grad: float32 [2, 1024], P(None, 'batch')
- mlp_in_grad: float32 [2, 1024, 4096], P(None, 'batch')
- mlp_in_bias_grad: float32 [2, 4096], P(None, 'batch')
- mlp_down_grad: float32 [2, 1024, 4096], P(None, 'batch')
- mlp_out_bias_grad: float32 [2, 1024], P(None, 'batch')
- norm_mean: float32 [], replicated
Inputs may be any that keep to these rules, and one draw needn't show every extreme that they name: Entry neighbours[g, j] names one of the 512 point rows of the block of 4 consecutive groups that holds g; entries may repeat. `lengths`: the value 256 occurs in every draw.
All inputs are finite; a program needn't handle non-finite values.
Results may differ from a plain program's by a relative error of at most 0.02.
Values may be sent and summed in bfloat16 or wider, within the bound.
A program may use at most 832 MiB of HBM per device.

v0:
```python
import functools
import math

import jax
import jax.numpy as jnp
from jax import lax
from jax.experimental import pallas as pl
from jax.experimental.pallas import tpu as pltpu
from jax.sharding import PartitionSpec as P

HD = 128
EPSILON = 1e-05
MASKED = -1e30
BF = jnp.bfloat16
F32 = jnp.float32
ALL = ("batch", "section")
MESH = pl.DeviceIdType.MESH
GATHER_WIDTH = 1024
AHEAD = 4
LOCAL = 1
SLOTS = 3
GATHERED = tuple(
    (4 * layer + index, start)
    for layer in range(2)
    for index, start in (
        [(0, 0), (0, 1024), (0, 2048), (1, 0)]
        + [(2 + which, chunk) for chunk in range(0, 2048, 1024) for which in range(2)]
    )
)


def mm(a, b):
    return jnp.dot(a, b, preferred_element_type=F32)


def mm_rows(a, b):
    return lax.dot_general(a, b, (((0,), (0,)), ((), ())), preferred_element_type=F32)


def mm_cols(a, b):
    return lax.dot_general(a, b, (((1,), (1,)), ((), ())), preferred_element_type=F32)


def unit_rows(values):
    centred = values - jnp.mean(values, axis=-1, keepdims=True)
    inverse = lax.rsqrt(jnp.mean(centred * centred, axis=-1, keepdims=True) + EPSILON)
    return centred * inverse, inverse


def norm_back(gradient, unit, inverse, gain):
    scaled = gradient * gain
    inner = (
        scaled
        - jnp.mean(scaled, axis=-1, keepdims=True)
        - unit * jnp.mean(scaled * unit, axis=-1, keepdims=True)
    )
    return inverse * inner, jnp.sum(gradient * unit, axis=0)


def heads_of(rows):
    return rows.reshape(rows.shape[0], -1, HD)


def softmax(q, k, valid):
    scores = jnp.einsum(
        "lhc,nhc->hln", heads_of(q), heads_of(k), preferred_element_type=F32
    ) * (1.0 / math.sqrt(HD))
    if valid is not None:
        scores = jnp.where(valid[None, None, :], scores, MASKED)
    grown = jnp.exp(scores - jnp.max(scores, axis=-1, keepdims=True))
    return grown / jnp.sum(grown, axis=-1, keepdims=True)


def attend(inputs, source, valid, gain_q, gain_kv, proj, out):
    unit_x, inv_x = unit_rows(inputs)
    queries_in = (unit_x * gain_q).astype(BF)
    unit_s, inv_s = unit_rows(source)
    keys_in = (unit_s * gain_kv).astype(BF)
    width = inputs.shape[1]
    q = mm(queries_in, proj[:, :width]).astype(BF)
    kv = mm(keys_in, proj[:, width:]).astype(BF)
    k, v = kv[:, :width], kv[:, width:]
    soft = softmax(q, k, valid)
    mixture = jnp.einsum("hln,nhc->lhc", soft.astype(BF), heads_of(v), preferred_element_type=F32)
    mixture = mixture.reshape(inputs.shape).astype(BF)
    result = (inputs + mm(mixture, out)).astype(BF)
    return result, (unit_x, inv_x, queries_in, unit_s, inv_s, keys_in, q, k, v, soft, mixture)


def attend_back(gradient, kept, gain_q, gain_kv, proj, out):
    unit_x, inv_x, queries_in, unit_s, inv_s, keys_in, q, k, v, soft, mixture = kept
    width = gradient.shape[1]
    scale = 1.0 / math.sqrt(HD)
    grad_mix = mm_cols(gradient, out).astype(BF)
    grad_soft = jnp.einsum(
        "lhc,nhc->hln", heads_of(grad_mix), heads_of(v), preferred_element_type=F32
    )
    inner = jnp.sum(soft * grad_soft, axis=-1, keepdims=True)
    grad_scores = (soft * (grad_soft - inner)).astype(BF)
    dq = jnp.einsum("hln,nhc->lhc", grad_scores, heads_of(k), preferred_element_type=F32) * scale
    dk = jnp.einsum("hln,lhc->nhc", grad_scores, heads_of(q), preferred_element_type=F32) * scale
    dv = jnp.einsum(
        "hln,lhc->nhc", soft.astype(BF), heads_of(grad_mix), preferred_element_type=F32
    )
    dq = dq.reshape(gradient.shape).astype(BF)
    dk = dk.reshape(-1, width).astype(BF)
    dv = dv.reshape(-1, width).astype(BF)
    grad_x, gain_q_grad = norm_back(mm_cols(dq, proj[:, :width]), unit_x, inv_x, gain_q)
    back_s = mm_cols(dk, proj[:, width : 2 * width]) + mm_cols(dv, proj[:, 2 * width :])
    grad_s, gain_kv_grad = norm_back(back_s, unit_s, inv_s, gain_kv)
    pairs = ((queries_in, dq), (keys_in, dk), (keys_in, dv), (mixture, gradient))
    return grad_x, grad_s, gain_q_grad, gain_kv_grad, pairs


def feed(inputs, gain, w_in, b_in, w_down, b_out):
    unit, inverse = unit_rows(inputs)
    lowered = (unit * gain).astype(BF)
    pre_act = mm(lowered, w_in) + b_in
    active = jax.nn.gelu(pre_act).astype(BF)
    result = (inputs + mm_cols(active, w_down) + b_out).astype(BF)
    return result, (unit, inverse, lowered, pre_act, active)


def feed_back(gradient, kept, gain, w_in, w_down):
    unit, inverse, lowered, pre_act, active = kept
    grad_act = mm(gradient, w_down)
    grad_pre = jax.vjp(jax.nn.gelu, pre_act)[1](grad_act)[0].astype(BF)
    grad_x, gain_grad = norm_back(mm_cols(grad_pre, w_in), unit, inverse, gain)
    bias_grad = jnp.sum(grad_pre.astype(F32), axis=0)
    out_grad = jnp.sum(gradient.astype(F32), axis=0)
    return grad_x, gain_grad, bias_grad, out_grad, ((lowered, grad_pre), (gradient, active))


def gelu_both(value):
    factor = math.sqrt(2.0 / math.pi)
    square = value * value
    bent = jnp.tanh(factor * value * (1.0 + 0.044715 * square))
    inner = factor * (1.0 + 3.0 * 0.044715 * square)
    half = 0.5 * (1.0 + bent)
    return value * half, half + 0.5 * value * (1.0 - bent * bent) * inner


def tiles(count, body, size=256):
    def step(index, carry):
        body(pl.ds(pl.multiple_of(index * size, size), size), index)
        return carry

    lax.fori_loop(0, count, step, 0)


def norm_into(source, gain, target):
    def step(index, carry):
        here = pl.ds(pl.multiple_of(index * 32, 32), 32)
        unit, _ = unit_rows(source[here, :].astype(F32))
        target[here, :] = (unit * gain).astype(BF)
        return carry

    lax.fori_loop(0, source.shape[0] // 32, step, 0)


def gather_kernel(*refs):
    cross_proj, cross_out, mlp_in, mlp_down, self_proj, self_out = refs[:6]
    latents_in, cot_all, points_in, near_in, length_in = refs[6:11]
    vec_parts = refs[11:16]
    section_at = lax.axis_index("section")
    batch_at = lax.axis_index("batch")
    x_at = lax.rem(section_at, 2)
    y_at = section_at // 2
    ins = (
        cross_proj,
        cross_out,
        mlp_in.at[0],
        mlp_down.at[0],
        self_proj,
        self_out,
        mlp_in.at[1],
        mlp_down.at[1],
    )
    count = len(ins)
    outs = refs[16 : 16 + count]
    rest = refs[16 + count :]
    gains, norm_out, mask_in, picks_out = rest[:4]
    kept_outs = rest[4:24]
    (
        u1,
        u2,
        u3,
        u4,
        grad_top,
        xq_c,
        sn_c,
        q_c,
        k_c,
        v_c,
        o_c,
        xn_s,
        q_s,
        k_s,
        v_s,
        o_s,
        src_in,
        lowered,
        before,
        active,
        x_in,
        cot_in,
        vec_in,
        vec_rows,
        slots,
        total_rows,
        part_out,
        part_in,
        vec_out,
        biases,
        plane,
        line_in,
    ) = rest[24:56]
    (own_sem, send, recv, kin_send, kin_recv, vec_sems) = rest[56:62]
    (slot_sems, kept_sems, plane_sems, line_sems, pair_sems, row_sems) = rest[62:]
    line = 4
    core = lax.rem(batch_at, 2)
    spot = batch_at // 2
    beside = section_at + 1 - 2 * x_at
    above = lax.rem(section_at + 2, 4)
    sibling = batch_at + 1 - 2 * core
    shard = ins[0].shape[0]
    place = section_at * 2 + core
    rows = x_in.shape[0]

    def down_line(step):
        return lax.rem(spot + step, line) * 2 + core

    def up_line(step):
        return lax.rem(spot + line - step, line) * 2 + core

    near_peers = []
    for turn in range(1, 8):
        other = lax.rem(place + turn, 8)
        near_peers.append((other // 2, spot * 2 + lax.rem(other, 2)))
    line_peers = [(section_at, down_line(step)) for step in range(1, line)]
    far_peers = [(section_at, down_line(step) + 1 - 2 * core) for step in range(1, line)]
    vec_peers = [(section_at, sibling)] + line_peers + far_peers
    peers = near_peers + line_peers + far_peers
    barrier = pltpu.get_barrier_semaphore()
    for peer in peers:
        pl.semaphore_signal(barrier, inc=1, device_id=peer, device_id_type=MESH)
    pl.semaphore_wait(barrier, len(peers))

    def spread(ref, owner, first, size):
        return ref.at[pl.ds(pl.multiple_of(owner * shard, shard), shard), pl.ds(first, size)]

    def is_feed(item):
        return item % 8 >= 4

    def source_of(item, first, size):
        index, start = GATHERED[item]
        if is_feed(item):
            first = pl.multiple_of(first + y_at * outs[index].shape[1], 128)
        return ins[index].at[:, pl.ds(first, size)]

    def piece(item):
        start = GATHERED[item][1]
        if is_feed(item):
            return pl.multiple_of(start + x_at * 512, 128), 512
        return pl.multiple_of(start + section_at * 256, 128), 256

    def own_line(item, way):
        first, size = piece(item)
        return pltpu.make_async_remote_copy(
            source_of(item, first, size),
            spread(outs[GATHERED[item][0]], batch_at, first, size),
            send.at[5 * way, item, 0],
            recv.at[0, item, 3 if way else 1],
            device_id=(section_at, batch_at + (-2 if way else 2)),
            device_id_type=MESH,
        )

    def onward_line(item, step, way):
        first, size = piece(item)
        ref = spread(outs[GATHERED[item][0]], up_line(step), first, size)
        return pltpu.make_async_remote_copy(
            ref,
            ref,
            send.at[0, item, step],
            recv.at[0, item, step - 1 if way else step + 1],
            device_id=(section_at, batch_at + (-2 if way else 2)),
            device_id_type=MESH,
        )

    def came_line(item, step):
        first, size = piece(item)
        ref = spread(outs[GATHERED[item][0]], up_line(step), first, size)
        return pltpu.make_async_remote_copy(
            ref,
            ref,
            send.at[0, item, step],
            recv.at[0, item, step],
            device_id=(section_at, sibling),
            device_id_type=MESH,
        )

    def start_line(item):
        @pl.when(spot < 3)
        def _():
            own_line(item, 0).start()

        @pl.when(spot > 0)
        def _():
            own_line(item, 1).start()

    def arrive_line(item, apart):
        @pl.when(spot >= apart)
        def _():
            came_line(item, apart).wait_recv()

            @pl.when(spot < 3)
            def _():
                onward_line(item, apart, 0).start()

            for copy in near(item, apart):
                copy.start()

        @pl.when(spot + apart <= 3)
        def _():
            came_line(item, 4 - apart).wait_recv()

            @pl.when(spot > 0)
            def _():
                onward_line(item, 4 - apart, 1).start()

            for copy in near(item, 4 - apart):
                copy.start()

    def sent_line(item):
        @pl.when(spot < 3)
        def _():
            own_line(item, 0).wait_send()

        @pl.when(spot > 0)
        def _():
            own_line(item, 1).wait_send()

        for apart in (1, 2, 3):

            @pl.when(jnp.logical_and(spot >= apart, spot < 3))
            def _():
                onward_line(item, apart, 0).wait_send()

            @pl.when(jnp.logical_and(spot + apart <= 3, spot > 0))
            def _():
                onward_line(item, 4 - apart, 1).wait_send()

        for step in (1, 2, 3):
            for copy in near(item, step):
                copy.wait_send()

    def plane_copy(item, step, way, low, wide, peer):
        ref = spread(outs[GATHERED[item][0]], up_line(step), low, wide)
        return pltpu.make_async_remote_copy(
            ref,
            ref,
            send.at[way, item, step],
            recv.at[way, item, step],
            device_id=(peer, batch_at),
            device_id_type=MESH,
        )

    def near(item, step):
        first, size = piece(item)
        copies = [plane_copy(item, step, 1, first, size, beside)]
        if not is_feed(item):
            copies.append(plane_copy(item, step, 2, first, size, above))
        return copies

    def far(item, step):
        start = GATHERED[item][1]
        by_y = pl.multiple_of(start + beside * 256, 128)
        by_x = pl.multiple_of(start + above * 256 + 128, 128)
        return [
            plane_copy(item, step, 3, by_y, 128, above),
            plane_copy(item, step, 4, by_x, 128, beside),
        ]

    def kin(item, step):
        index, start = GATHERED[item]
        if step == 0:
            source = source_of(item, start, GATHER_WIDTH)
        else:
            source = spread(outs[index], up_line(step), start, GATHER_WIDTH)
        return pltpu.make_async_remote_copy(
            source,
            spread(outs[index], up_line(step), start, GATHER_WIDTH),
            kin_send.at[item, step],
            kin_recv.at[item, step],
            device_id=(section_at, sibling),
            device_id_type=MESH,
        )

    def own(item):
        index, start = GATHERED[item]
        return pltpu.make_async_copy(
            source_of(item, start, GATHER_WIDTH),
            spread(outs[index], batch_at, start, GATHER_WIDTH),
            own_sem.at[item],
        )

    def vec_copy(which):
        return pltpu.make_async_remote_copy(
            vec_in,
            vec_out.at[batch_at],
            vec_sems.at[0, which],
            vec_sems.at[1, which],
            device_id=vec_peers[which],
            device_id_type=MESH,
        )

    def slot_copy(item):
        index, start = GATHERED[item]
        return pltpu.make_async_copy(
            outs[index].at[:, pl.ds(start, GATHER_WIDTH)],
            slots.at[item % SLOTS],
            slot_sems.at[item % SLOTS],
        )

    def near_norm(turn):
        return pltpu.make_async_remote_copy(
            plane.at[8],
            plane.at[place],
            plane_sems.at[0, turn],
            plane_sems.at[1, turn],
            device_id=near_peers[turn],
            device_id_type=MESH,
        )

    def far_norm(step):
        return pltpu.make_async_remote_copy(
            line_in.at[4],
            line_in.at[spot],
            line_sems.at[0, step],
            line_sems.at[1, step],
            device_id=line_peers[step],
            device_id_type=MESH,
        )

    def rows_over(layer):
        return pltpu.make_async_remote_copy(
            lowered.at[layer, pl.ds(0, rows)],
            lowered.at[layer, pl.ds(rows, rows)],
            pair_sems.at[0, layer, 0],
            pair_sems.at[1, layer, 0],
            device_id=(above, batch_at),
            device_id_type=MESH,
        )

    def part_over(layer):
        return pltpu.make_async_remote_copy(
            part_out.at[layer],
            part_in.at[layer],
            pair_sems.at[0, layer, 1],
            pair_sems.at[1, layer, 1],
            device_id=(above, batch_at),
            device_id_type=MESH,
        )

    steps = range(1, line)
    total = len(GATHERED)
    started = []

    def launch(copies):
        for copy in copies:
            copy.start()
        started.extend(copies)

    kept = (
        (u1, u2, u3, u4, grad_top)
        + (xq_c, sn_c, q_c, k_c, v_c, o_c)
        + (xn_s, q_s, k_s, v_s, o_s)
        + (src_in, lowered, before, active)
    )
    names = {id(ref): place for place, ref in enumerate(kept)}

    def keep(*chosen):
        for ref in chosen:
            index = names[id(ref)]
            pltpu.make_async_copy(ref, kept_outs[index], kept_sems.at[index]).start(priority=LOCAL)

    def row(index):
        return gains[index : index + 1, :]

    def project(source, target, slot):
        def tile(columns, _):
            target[:, columns] = mm(source[...], slots[slot, :, columns]).astype(BF)

        tiles(2, tile, 512)

    def heads(q, k, v, o, masked):
        def head(index, carry):
            here = pl.ds(pl.multiple_of(index * HD, HD), HD)
            scores = mm_cols(q[:, here], k[:, here]) * (1.0 / math.sqrt(HD))
            if masked:
                scores = jnp.where(mask_in[...] > 0.0, scores, MASKED)
            grown = jnp.exp(scores - jnp.max(scores, axis=-1, keepdims=True))
            soft = grown / jnp.sum(grown, axis=-1, keepdims=True)
            o[:, here] = mm(soft.astype(BF), v[:, here]).astype(BF)
            return carry

        lax.fori_loop(0, q.shape[1] // HD, head, 0)

    def close_attention(inputs, o, target, slot):
        def tile(columns, _):
            target[:, columns] = (
                inputs[:, columns].astype(F32) + mm(o[...], slots[slot, :, columns])
            ).astype(BF)

        tiles(2, tile, 512)

    def feed_up(layer, chunk, slot):
        def tile(columns, index):
            first = chunk * GATHER_WIDTH + index * 512
            there = pl.ds(pl.multiple_of(first, 512), 512)
            lanes = pl.ds(pl.multiple_of(y_at * 2048 + first, 512), 512)
            value = mm(lowered[layer], slots[slot, :, columns]) + biases[layer : layer + 1, lanes]
            active_part, slope = gelu_both(value)
            before[layer, :, there] = slope
            active[layer, :, there] = active_part.astype(BF)

        tiles(2, tile, 512)

    def feed_down(layer, chunk, slot):
        chosen = pl.ds(chunk * GATHER_WIDTH, GATHER_WIDTH)

        def tile(columns, _):
            value = mm_cols(active[layer, :, chosen], slots[slot, columns, :])
            if chunk == 0:
                total_rows[:, columns] = value
            else:
                value = total_rows[:, columns] + value
                total_rows[:, columns] = value
                part_out[layer, :, columns] = value[rows:].astype(BF)

        tiles(2, tile, 512)

    def feed_close(layer):
        inputs, target = (u1, u3)[layer], (u2, u4)[layer]
        part_over(layer).wait_recv()

        def tile(columns, _):
            target[:, columns] = (
                inputs[:, columns].astype(F32)
                + (total_rows[0:rows, columns] + part_in[layer, :, columns].astype(F32))
                + gains[5 + layer : 6 + layer, columns]
            ).astype(BF)

        tiles(2, tile, 512)
        keep(target)

    def work(item):
        slot_copy(item).wait()
        slot = item % SLOTS
        layer, stage = item // 8, item % 8
        inputs = (x_in, u2)[layer]
        middle = (u1, u3)[layer]
        q, k, v, o = ((q_c, k_c, v_c, o_c), (q_s, k_s, v_s, o_s))[layer]
        if stage == 0:
            if layer == 0:
                norm_into(x_in, row(0), xq_c)
                norm_into(src_in, row(1), sn_c)
                keep(xq_c, sn_c)
            else:
                feed_close(0)
                norm_into(u2, row(2), xn_s)
                keep(xn_s)
            project((xq_c, xn_s)[layer], q, slot)
        elif stage == 1:
            project((sn_c, xn_s)[layer], k, slot)
        elif stage == 2:
            project((sn_c, xn_s)[layer], v, slot)
            heads(q, k, v, o, layer == 0)
            keep(q, k, v, o)
        elif stage == 3:
            close_attention(inputs, o, middle, slot)
            norm_into(middle, row(3 + layer), lowered.at[layer, pl.ds(0, rows)])
            launch([rows_over(layer)])
            keep(middle)
        elif stage % 2 == 0:
            if stage == 4:
                rows_over(layer).wait_recv()
            feed_up(layer, (stage - 4) // 2, slot)
        else:
            feed_down(layer, (stage - 4) // 2, slot)
            if stage == 7:
                launch([part_over(layer)])

    for item in range(AHEAD):
        start_line(item)
    here = pl.ds(pl.multiple_of(section_at * rows, rows), rows)
    row_copies = [
        pltpu.make_async_copy(latents_in.at[here], x_in, row_sems.at[0]),
        pltpu.make_async_copy(cot_all.at[here], cot_in, row_sems.at[1]),
    ]
    for copy in row_copies:
        copy.start()
    cross_gain, self_gain, feed_gain, out_bias, in_bias = vec_parts
    vec_rows[...] = jnp.zeros_like(vec_rows)
    vec_rows[0:2, :] = cross_gain[...].astype(F32)
    vec_rows[2:3, :] = self_gain[...].astype(F32)
    vec_rows[3:5, :] = feed_gain[...].astype(F32)
    vec_rows[5:7, :] = out_bias[...].astype(F32)
    bias_rows = in_bias[...].astype(F32)
    for layer in range(2):
        for part_at in range(4):
            index = 7 + 4 * layer + part_at
            vec_rows[index : index + 1, :] = bias_rows[
                layer : layer + 1, part_at * 128 : part_at * 128 + 128
            ]
    vec_in[...] = vec_rows[...].astype(BF)
    vec_out[batch_at] = vec_in[...]
    for which in range(7):
        vec_copy(which).start()
    lanes = lax.broadcasted_iota(jnp.int32, (1, rows), 1)
    length = length_in[pl.ds(section_at, 1), :]
    mask_in[...] = jnp.where(lanes < length, 1.0, 0.0)
    point_at = lax.broadcasted_iota(jnp.int32, (points_in.shape[0], rows), 0)
    wanted = near_in[pl.ds(section_at, 1), :]
    picks = jnp.where(point_at == wanted, 1.0, 0.0)
    picks_out[...] = picks.astype(BF)
    turned = picks.T.astype(BF)

    def source_tile(columns, _):
        src_in[:, columns] = mm(turned, points_in[:, columns]).astype(BF)

    tiles(2, source_tile, 512)
    keep(src_in)
    for copy in row_copies:
        copy.wait()
    for moment in range(-2, total + 4):
        if moment + 2 + AHEAD < total:
            start_line(moment + 2 + AHEAD)
        for apart in (1, 2, 3):
            if 0 <= moment + 3 - apart < total:
                arrive_line(moment + 3 - apart, apart)
        if 0 <= moment < total:
            own(moment).start(priority=LOCAL)
            launch([kin(moment, 0)])
        if 0 <= moment - 1 < total:
            for step in steps:
                if is_feed(moment - 1):
                    near(moment - 1, step)[0].wait_recv()
                    launch([kin(moment - 1, step)])
                else:
                    for copy, onward in zip(near(moment - 1, step), far(moment - 1, step)):
                        copy.wait_recv()
                        launch([onward])
        if 0 <= moment - 2 < total and not is_feed(moment - 2):
            for step in steps:
                for copy in far(moment - 2, step):
                    copy.wait_recv()
                launch([kin(moment - 2, step)])
        if moment == 2:
            for which in range(7):
                vec_copy(which).wait()
            for owner in range(8):
                values = vec_out[owner].astype(F32)
                gains[:, owner * 128 : owner * 128 + 128] = values
                for layer in range(2):
                    for part_at in range(4):
                        first = owner * 512 + part_at * 128
                        index = 7 + 4 * layer + part_at
                        biases[layer : layer + 1, first : first + 128] = values[index : index + 1]
        if 0 <= moment - 4 < total:
            work(moment - 4)
        if 0 <= moment - 3 < total:
            own(moment - 3).wait()
            for step in range(line):
                kin(moment - 3, step).wait_recv()
            slot_copy(moment - 3).start(priority=LOCAL)
    keep(lowered, before, active)
    feed_close(1)

    def square(index, carry):
        here = pl.ds(pl.multiple_of(index * 32, 32), 32)
        values = u4[here, :].astype(F32)
        return carry + jnp.sum(values * values, axis=0, keepdims=True)

    squares = lax.fori_loop(0, u4.shape[0] // 32, square, jnp.zeros((1, u4.shape[1]), F32))
    mean = jnp.sum(squares, axis=1, keepdims=True) / (u4.shape[0] * u4.shape[1])
    group_norm = jnp.sqrt(mean + EPSILON)
    plane[8] = jnp.broadcast_to(group_norm, plane.shape[1:])
    for turn in range(7):
        near_norm(turn).start()
    plane[place] = plane[8]
    for turn in range(7):
        near_norm(turn).wait()
    line_in[4] = jnp.sum(plane[0:8], axis=0)
    for step in range(3):
        far_norm(step).start()
    line_in[spot] = line_in[4]
    for step in range(3):
        far_norm(step).wait()
    norm_mean = jnp.sum(line_in[0:4], axis=0) / 32.0
    norm_out[...] = norm_mean
    ratio = norm_mean[0:1, 0:1] / group_norm

    def top(index, carry):
        here = pl.ds(pl.multiple_of(index * 32, 32), 32)
        grad_top[here, :] = (
            cot_in[here, :].astype(F32) + ratio * u4[here, :].astype(F32)
        ).astype(BF)
        return carry

    lax.fori_loop(0, u4.shape[0] // 32, top, 0)
    keep(grad_top)
    for index, ref in enumerate(kept):
        pltpu.make_async_copy(ref, kept_outs[index], kept_sems.at[index]).wait()
    for item in range(total):
        sent_line(item)
    for copy in started:
        copy.wait_send()


def gather_forward(blocks, latents, cotangent, points, near, lengths, vectors):
    width = latents.shape[1]
    rows = near.shape[1]
    half = blocks[2].shape[2] // 2
    widths = (3 * width, width, half, half) * 2
    total = len(GATHERED)
    anywhere = pl.BlockSpec(memory_space=pl.ANY)
    vmem = pl.BlockSpec(memory_space=pltpu.VMEM)
    plain = ((rows, width), BF)
    kept = [plain] * 17 + [
        ((2, 2 * rows, width), BF),
        ((2, 2 * rows, half), F32),
        ((2, 2 * rows, half), BF),
    ]
    dma = pltpu.SemaphoreType.DMA
    return pl.pallas_call(
        gather_kernel,
        out_shape=[jax.ShapeDtypeStruct((width, size), BF) for size in widths]
        + [
            jax.ShapeDtypeStruct((16, width), F32),
            jax.ShapeDtypeStruct((8, 128), F32),
            jax.ShapeDtypeStruct((1, rows), F32),
            jax.ShapeDtypeStruct((points.shape[0], rows), BF),
        ]
        + [jax.ShapeDtypeStruct(*one) for one in kept],
        in_specs=[anywhere] * (len(blocks) + 2) + [vmem] * 8,
        out_specs=[anywhere] * len(widths) + [vmem] * 4 + [anywhere] * len(kept),
        scratch_shapes=[pltpu.VMEM(*one) for one in kept]
        + [
            pltpu.VMEM((rows, width), BF),
            pltpu.VMEM((rows, width), BF),
            pltpu.VMEM((16, 128), BF),
            pltpu.VMEM((16, 128), F32),
            pltpu.VMEM((SLOTS, width, GATHER_WIDTH), BF),
            pltpu.VMEM((2 * rows, width), F32),
            pltpu.VMEM((2, rows, width), BF),
            pltpu.VMEM((2, rows, width), BF),
            pltpu.VMEM((8, 16, 128), BF),
            pltpu.VMEM((2, 2 * half), F32),
            pltpu.VMEM((9, 8, 128), F32),
            pltpu.VMEM((5, 8, 128), F32),
            dma((total,)),
            dma((6, total, 4)),
            dma((5, total, 4)),
            dma((total, 4)),
            dma((total, 4)),
            dma((2, 7)),
            dma((SLOTS,)),
            dma((len(kept),)),
            dma((2, 7)),
            dma((2, 3)),
            dma((2, 2, 2)),
            dma((2,)),
        ],
        compiler_params=pltpu.CompilerParams(
            collective_id=1, has_side_effects=True, vmem_limit_bytes=56 * 2**20
        ),
        cost_estimate=pl.CostEstimate(
            flops=2 * rows * width * sum(widths), bytes_accessed=2**27, transcendentals=2**21
        ),
    )(*blocks, latents, cotangent, points, near, lengths, *vectors)


ITEM_COUNT = 16
WINDOWS = 4
STAGES = 3


def reduce_kernel(*refs):
    total = ITEM_COUNT
    (
        proj_c,
        out_c,
        in_0,
        down_0,
        proj_s,
        out_s,
        in_1,
        down_1,
        u1_in,
        u2_in,
        u3_in,
        last_ref,
        top_in,
        xq_c,
        sn_c,
        q_c,
        k_c,
        v_c,
        o_c,
        xn_s,
        q_s,
        k_s,
        v_s,
        o_s,
        lowered,
        before,
        active,
        latents_in,
        src_in,
        gains,
        mask_in,
        picks_in,
    ) = refs[:32]
    (up_out, down_out, proj_out_c, proj_out_s, end_out_c, end_out_s) = refs[32:38]
    (last_out, first_out, point_out, small_out) = refs[38:42]
    (grads_h, kin_lf, kin_la, kin_rf, kin_ra) = refs[42:47]
    (
        lwin_f,
        lwin_a,
        raw,
        rwin,
        stage,
        merged_f,
        merged_a,
        passing,
        lined_f,
        lined_a,
        crossed_f,
        crossed_a,
        pair,
        slope,
        rows_sum,
        hbuf,
        slots,
        qb,
        kb,
        vb,
        dob,
        dqkv,
        part_out,
        part_in,
        grad,
        ub,
        point_in,
        point_sum,
        small_in,
        small_sum,
    ) = refs[47:77]
    (
        kin_l_sems,
        kin_r_sems,
        raw_sems,
        win_sems,
        xy_sems,
        line_send,
        line_recv,
        cross_sems,
        out_sems,
        own_sems,
        lat_sems,
        far_sems,
        lat_own,
        point_sems,
        deal_sems,
        point_own,
        small_sems,
        pair_sems,
        slot_sems,
        h_sem,
        save_sems,
        act_sems,
    ) = refs[77:]
    section_at = lax.axis_index("section")
    batch_at = lax.axis_index("batch")
    core = lax.rem(batch_at, 2)
    spot = batch_at // 2
    x_at = lax.rem(section_at, 2)
    y_at = section_at // 2
    beside = section_at + 1 - 2 * x_at
    above = lax.rem(section_at + 2, 4)
    across = lax.rem(beside + 2, 4)
    sibling = batch_at + 1 - 2 * core
    flat = (beside, above)
    bits = (x_at, y_at)
    rows, width = 256, 1024

    peers = [(beside, batch_at), (above, batch_at), (across, batch_at), (section_at, sibling)]
    peers += [(section_at, lax.rem(spot + step, 4) * 2 + core) for step in (1, 2, 3)]
    barrier = pltpu.get_barrier_semaphore()
    for peer in peers:
        pl.semaphore_signal(barrier, inc=1, device_id=peer, device_id_type=MESH)
    pl.semaphore_wait(barrier, len(peers))

    def remote(source, target, sems, where, peer):
        return pltpu.make_async_remote_copy(
            source,
            target,
            sems.at[(0, *where)],
            sems.at[(1, *where)],
            device_id=peer,
            device_id_type=MESH,
        )

    feed_left = (pair, lowered.at[1], pair, lowered.at[0])
    feed_right = (active.at[1], slope, active.at[0], slope)
    att_left = (o_s, xn_s, xn_s, xn_s, o_c, xq_c, sn_c, sn_c)
    att_right = tuple(
        ref
        for turn in range(2)
        for ref in (grads_h.at[turn], dqkv.at[0], dqkv.at[1], dqkv.at[2])
    )

    def columns(spot_of, parity):
        return pl.ds(pl.multiple_of((2 * spot_of + parity) * 128, 128), 128)

    def kin_lefts(feed, job):
        source, target = (feed_left, kin_lf) if feed else (att_left, kin_la)
        return [
            remote(
                source[job].at[:, columns(part, 1 - core)],
                target.at[job, part],
                kin_l_sems,
                (job if feed else 4 + job, part),
                (section_at, sibling),
            )
            for part in range(4)
        ]

    def kin_right(feed, job, chunk):
        if feed:
            here = pl.ds(chunk * 1024, 1024)
            source, target = feed_right[job].at[:, here], kin_rf.at[job, :, here]
        else:
            source, target = att_right[job], kin_ra.at[job]
        where = (2 * job + chunk if feed else 8 + job,)
        return remote(source, target, kin_r_sems, where, (section_at, sibling))

    def item_of(index):
        turn, inner = index // 8, index % 8
        if inner < 4:
            return True, 2 * turn + inner // 2, inner % 2
        return False, 4 * turn + inner - 4, 0

    def window_copies(index):
        feed, job, chunk = item_of(index)
        slot = index % WINDOWS
        size = 512 if feed else 256
        if feed:
            here = pl.ds(chunk * 1024, 1024)
            sources = (feed_right[job].at[:, here], kin_rf.at[job, :, here])
        else:
            sources = (att_right[job], kin_ra.at[job])
        return [
            pltpu.make_async_copy(
                sources[whose],
                rwin.at[slot, pl.ds(whose * size, size)],
                win_sems.at[slot, whose],
            )
            for whose in range(2)
        ]

    def raw_copies(index, part):
        feed, job, _ = item_of(index)
        size = 512 if feed else 256
        own_left = (feed_left if feed else att_left)[job]
        kin_left = (kin_lf if feed else kin_la).at[job]
        sources = (own_left.at[:, columns(part, core)], kin_left.at[part])
        return [
            pltpu.make_async_copy(
                source, raw.at[part, whose, pl.ds(0, size)], raw_sems.at[part, whose]
            )
            for whose, source in enumerate(sources)
        ]

    def raw_start(index):
        feed, job, chunk = item_of(index)
        if chunk == 0:
            for copy in kin_lefts(feed, job):
                copy.wait_recv()
            for part in range(4):
                for copy in raw_copies(index, part):
                    copy.start(priority=LOCAL)

    def load(index):
        feed, job, chunk = item_of(index)
        kin_right(feed, job, chunk).wait_recv()
        for copy in window_copies(index):
            copy.start(priority=LOCAL)
        if chunk == 0:
            size = 512 if feed else 256
            target = (lwin_f if feed else lwin_a).at[job]
            for part in range(4):
                for whose, copy in enumerate(raw_copies(index, part)):
                    copy.wait()
                    place = raw.at[part, whose, pl.ds(0, size)]
                    target[part, :, whose * size : whose * size + size] = place[...].T
        if index + 1 < total:
            raw_start(index + 1)

    def is_feed(item):
        return lax.rem(item, 8) < 4

    def feed_job(item):
        return 2 * (item // 8) + lax.rem(item, 8) // 2

    def att_job(item):
        return 4 * (item // 8) + lax.rem(item, 8) - 4

    def loaded(slot, feed):
        size = 512 if feed else 256
        for whose in range(2):
            source = kin_rf.at[0, :, pl.ds(0, 1024)] if feed else kin_ra.at[0]
            pltpu.make_async_copy(
                source, rwin.at[slot, pl.ds(whose * size, size)], win_sems.at[slot, whose]
            ).wait()

    def by_kind(item, action):
        pl.when(is_feed(item))(functools.partial(action, item, True))
        pl.when(jnp.logical_not(is_feed(item)))(functools.partial(action, item, False))

    def merged_of(item, feed):
        return merged_f.at[lax.rem(item, 4)] if feed else merged_a.at[att_job(item)]

    def passing_of(item, feed, slot):
        ref = passing.at[lax.rem(item, 8), slot]
        return ref if feed else ref.at[:, pl.ds(0, 512)]

    def lined_of(item, feed):
        return lined_f.at[lax.rem(item, 4)] if feed else lined_a.at[att_job(item)]

    def crossed_of(item, feed):
        return crossed_f.at[lax.rem(item, 4)] if feed else crossed_a.at[att_job(item)]

    def products(item, choice, store):
        slot = lax.rem(item, WINDOWS)

        def quarter(index, carry):
            here = pl.ds(pl.multiple_of(index * 256, 256), 256)
            bit = choice[0] + index * (choice[1] - choice[0])
            first = pl.multiple_of(index * 512 + bit * 256, 256)
            left = lwin_a[att_job(item)].reshape(512, 512)
            right = rwin[slot, 0:512, pl.ds(first, 256)]
            tile = jnp.dot(left, right, preferred_element_type=F32).reshape(4, 128, 256)
            store(pl.ds(0, 4), here, tile)
            return carry

        lax.fori_loop(0, 2, quarter, 0)

    def xy_copies(item):
        return [
            remote(
                stage.at[lax.rem(att_job(item), STAGES), :, :, pl.ds(side * 256, 256)],
                merged_a.at[att_job(item), :, :, pl.ds(side * 256, 256)],
                xy_sems,
                (att_job(item), side),
                (flat[side], batch_at),
            )
            for side in range(2)
        ]

    def xy_sent(item):
        for copy in xy_copies(item):
            copy.wait_send()

    def line_copy(item, feed, dest, place, rightward):
        step = 1 if rightward else -1
        slot = 4 if not rightward and place - 1 == dest else dest
        return pltpu.make_async_remote_copy(
            merged_of(item, feed).at[dest],
            passing_of(item, feed, slot),
            line_send.at[item, dest],
            line_recv.at[item, slot],
            device_id=(section_at, batch_at + 2 * step),
            device_id_type=MESH,
        )

    def line_wait(item, feed, slot):
        pltpu.make_async_remote_copy(
            merged_of(item, feed).at[0],
            passing_of(item, feed, slot),
            line_send.at[item, 0],
            line_recv.at[item, slot],
            device_id=(section_at, sibling),
            device_id_type=MESH,
        ).wait_recv()

    def line_sent(item, feed):
        for step in (1, 2, 3):
            dest = lax.rem(spot + step, 4)
            pltpu.make_async_remote_copy(
                merged_of(item, feed).at[dest],
                passing_of(item, feed, 0),
                line_send.at[item, dest],
                line_recv.at[item, 0],
                device_id=(section_at, sibling),
                device_id_type=MESH,
            ).wait_send()

    def outset(item, feed):
        @pl.when(spot == 0)
        def _():
            for dest in (3, 2, 1):
                line_copy(item, feed, dest, 0, True).start()

        @pl.when(spot == 3)
        def _():
            for dest in (0, 1, 2):
                line_copy(item, feed, dest, 3, False).start()

    def drained(item, feed):
        line_sent(item, feed)
        if feed:
            feed_out(item, up_out).wait()
            feed_own(item, up_out).wait()
        else:
            for side in range(2):
                att_out(item, side, end_out_s, 0).wait()
                att_own(item, side, end_out_s, 0).wait()

    def offer(item, feed):
        slot = lax.rem(item, WINDOWS)
        loaded(slot, feed)
        if feed:

            @pl.when(item >= 8)
            def _():
                drained(item - 8, True)

            target = merged_of(item, True)

            def tile(index, carry):
                here = pl.ds(pl.multiple_of(index * 256, 256), 256)
                left = lwin_f[feed_job(item)].reshape(512, 1024)
                right = rwin[slot, :, here]
                value = jnp.dot(left, right, preferred_element_type=F32)
                target[:, :, here] = value.reshape(4, 128, 256).astype(BF)
                return carry

            lax.fori_loop(0, 4, tile, 0)
            outset(item, True)
        else:

            @pl.when(lax.rem(item, 8) >= 4 + STAGES)
            def _():
                xy_sent(item - STAGES)

            @pl.when(jnp.logical_and(item >= 12, lax.rem(item, 8) < 4 + STAGES))
            def _():
                xy_sent(item - STAGES - 4)

            def store(blocks, here, tile):
                stage[lax.rem(att_job(item), STAGES), blocks, :, here] = tile.astype(BF)

            products(item, (1 - x_at, 1 - y_at), store)
            for copy in xy_copies(item):
                copy.start()

    def take(item):
        for copy in xy_copies(item):
            copy.wait_recv()
        target = merged_a.at[att_job(item)]

        def store(blocks, here, tile):
            target[blocks, :, here] = (tile + target[blocks, :, here].astype(F32)).astype(BF)

        products(item, bits, store)
        outset(item, False)

    def first(item):
        pl.when(jnp.logical_not(is_feed(item)))(functools.partial(take, item))

    def relay(item, feed, dest, place, rightward):
        line_wait(item, feed, dest)
        target = merged_of(item, feed)
        arrived = passing_of(item, feed, dest)
        target[dest] = (target[dest].astype(F32) + arrived[...].astype(F32)).astype(BF)
        line_copy(item, feed, dest, place, rightward).start()

    def second_of(item, feed):
        @pl.when(spot == 1)
        def _():
            for dest in (3, 2):
                relay(item, feed, dest, 1, True)

        @pl.when(spot == 2)
        def _():
            for dest in (0, 1):
                relay(item, feed, dest, 2, False)

    def third_of(item, feed):
        @pl.when(spot == 1)
        def _():
            relay(item, feed, 0, 1, False)

        @pl.when(spot == 2)
        def _():
            relay(item, feed, 3, 2, True)

    def second(item):
        by_kind(item, second_of)

    def third(item):
        by_kind(item, third_of)

    def feed_cross(item):
        return remote(
            lined_of(item, True),
            crossed_of(item, True),
            cross_sems,
            (item, 0),
            (beside, batch_at),
        )

    def cross_copy(item, side):
        here = pl.ds(side * 256, 256)
        return remote(
            lined_of(item, False).at[:, here],
            crossed_of(item, False).at[:, here],
            cross_sems,
            (item, side),
            (flat[1 - side], batch_at),
        )

    def layer_of(item):
        return 1 - item // 8

    def feed_place(item, target):
        base = y_at * 2048 + lax.rem(item, 2) * 1024
        return target.at[layer_of(item), :, pl.ds(pl.multiple_of(base, 1024), 1024)]

    def feed_out(item, target):
        return remote(
            lined_of(item, True),
            feed_place(item, target),
            out_sems,
            (item, 0),
            (above, batch_at),
        )

    def feed_own(item, target):
        return pltpu.make_async_copy(
            lined_of(item, True), feed_place(item, target), own_sems.at[item, 0]
        )

    def feed_write(item):
        @pl.when(lax.rem(item, 8) < 2)
        def _():
            feed_out(item, down_out).start()
            feed_own(item, down_out).start(priority=LOCAL)

        @pl.when(lax.rem(item, 8) >= 2)
        def _():
            feed_out(item, up_out).start()
            feed_own(item, up_out).start(priority=LOCAL)

    def att_place(item, side, target, inner):
        base = inner * 1024 + side * 512 + bits[side] * 256
        return target.at[:, pl.ds(pl.multiple_of(base, 256), 256)]

    def att_out(item, side, target, inner):
        return remote(
            lined_of(item, False).at[:, pl.ds(side * 256, 256)],
            att_place(item, side, target, inner),
            out_sems,
            (item, side),
            (flat[side], batch_at),
        )

    def att_own(item, side, target, inner):
        return pltpu.make_async_copy(
            lined_of(item, False).at[:, pl.ds(side * 256, 256)],
            att_place(item, side, target, inner),
            own_sems.at[item, side],
        )

    def att_write(item):
        inner = lax.rem(item, 8) - 5
        for turn, proj, end in ((0, proj_out_s, end_out_s), (1, proj_out_c, end_out_c)):

            @pl.when(jnp.logical_and(item // 8 == turn, inner >= 0))
            def _():
                for side in range(2):
                    att_out(item, side, proj, inner).start()
                    att_own(item, side, proj, inner).start(priority=LOCAL)

            @pl.when(jnp.logical_and(item // 8 == turn, inner < 0))
            def _():
                for side in range(2):
                    att_out(item, side, end, 0).start()
                    att_own(item, side, end, 0).start(priority=LOCAL)

    def close_of(item, feed):
        for place in range(4):

            @pl.when(spot == place)
            def _():
                value = merged_of(item, feed)[place].astype(F32)
                if place > 0:
                    line_wait(item, feed, place)
                    value += passing_of(item, feed, place)[...].astype(F32)
                if place < 3:
                    line_wait(item, feed, 4)
                    value += passing_of(item, feed, 4)[...].astype(F32)
                lined_of(item, feed)[...] = value.astype(BF)

        if feed:
            feed_cross(item).start()
        else:
            for side in range(2):
                cross_copy(item, side).start()

    def close(item):
        by_kind(item, close_of)

    def finish_of(item, feed):
        if feed:
            feed_cross(item).wait()
        else:
            for side in range(2):
                cross_copy(item, side).wait()
        target = lined_of(item, feed)
        target[...] = (
            target[...].astype(F32) + crossed_of(item, feed)[...].astype(F32)
        ).astype(BF)
        if feed:
            feed_write(item)
        else:
            att_write(item)

    def finish(item):
        by_kind(item, finish_of)

    def small_copy(phase):
        if phase == 0:
            peer = (section_at, sibling)
        elif phase < 3:
            peer = (flat[phase - 1], batch_at)
        else:
            peer = (section_at, lax.rem(spot + phase - 2, 4) * 2 + core)
        return remote(
            small_sum.at[min(phase, 3)], small_in.at[phase], small_sems, (phase,), peer
        )

    quarter_rows = pair.shape[0] // 4

    def point_copy(which):
        peer = (beside, above, across)[which]
        return remote(
            pair.at[pl.ds(pl.multiple_of(peer * quarter_rows, 128), quarter_rows)],
            point_in.at[which],
            point_sems,
            (which,),
            (peer, batch_at),
        )

    def point_place():
        return point_out.at[pl.ds(pl.multiple_of(section_at * quarter_rows, 128), quarter_rows)]

    def point_deal(which):
        peer = (beside, above, across)[which]
        return remote(point_sum, point_place(), deal_sems, (which,), (peer, batch_at))

    def point_local():
        return pltpu.make_async_copy(point_sum, point_place(), point_own.at[0])

    pairs = ((last_ref, last_out), (grad, first_out))

    def lat_copy(which, way):
        source, target = pairs[which]
        return remote(
            source,
            target.at[pl.ds(pl.multiple_of(section_at * rows, rows), rows)],
            lat_sems,
            (which, way),
            (flat[way], batch_at),
        )

    def lat_far(which, way):
        target = pairs[which][1]
        low = flat[way] * rows + way * (rows // 2)
        part = target.at[pl.ds(pl.multiple_of(low, rows // 2), rows // 2)]
        return remote(part, part, far_sems, (which, way), (flat[1 - way], batch_at))

    def lat_local(which):
        source, target = pairs[which]
        return pltpu.make_async_copy(
            source,
            target.at[pl.ds(pl.multiple_of(section_at * rows, rows), rows)],
            lat_own.at[which],
        )

    def lat_start(which):
        lat_local(which).start(priority=LOCAL)
        for way in range(2):
            lat_copy(which, way).start()

    def lat_onward(which):
        for way in range(2):
            lat_copy(which, way).wait_recv()
            lat_far(which, way).start()

    loads = []
    for turn, (proj, out, up, down) in enumerate(
        ((proj_s, out_s, in_1, down_1), (proj_c, out_c, in_0, down_0))
    ):
        for chunk in range(2):
            loads += [down.at[:, pl.ds(chunk * 1024, 1024)], up.at[:, pl.ds(chunk * 1024, 1024)]]
        loads.append(out)
        loads += [proj.at[:, pl.ds(which * 1024, 1024)] for which in range(3)]

    def slot_copy(index):
        return pltpu.make_async_copy(loads[index], slots.at[index % 2], slot_sems.at[index % 2])

    def opened(index):
        slot_copy(index).wait()
        return index % 2

    def closed(index):
        if index + 2 < len(loads):
            slot_copy(index + 2).start(priority=LOCAL)

    def h_copy(index):
        layer, chunk = 1 - index // 2, index % 2
        return pltpu.make_async_copy(
            before.at[layer, :, pl.ds(chunk * 1024, 1024)], hbuf, h_sem.at[0]
        )

    def pair_over(turn):
        return remote(
            pair.at[pl.ds(0, rows)],
            pair.at[pl.ds(rows, rows)],
            pair_sems,
            (turn, 0),
            (above, batch_at),
        )

    def part_over(turn):
        return remote(
            part_out.at[turn], part_in.at[turn], pair_sems, (turn, 1), (above, batch_at)
        )

    def grad_saved(turn):
        return pltpu.make_async_copy(grad, grads_h.at[turn], save_sems.at[0])

    def act_copies(turn):
        chosen = ((q_s, k_s, v_s), (q_c, k_c, v_c))[turn]
        return [
            pltpu.make_async_copy(source, target, act_sems.at[index])
            for index, (source, target) in enumerate(zip(chosen, (qb, kb, vb)))
        ]

    def row_copy(index):
        if index == 3:
            source = latents_in.at[pl.ds(pl.multiple_of(section_at * rows, rows), rows)]
        else:
            source = (u3_in, u2_in, u1_in)[index]
        return pltpu.make_async_copy(source, ub, act_sems.at[3])

    def small_row(index, value):
        small_sum[0, index : index + 1, :] = value

    def open_pair(turn):
        pair[0:rows, :] = grad[...]
        pair_over(turn).start()

    def pair_ready(turn):
        pair_over(turn).wait()
        for copy in kin_lefts(True, 2 * turn):
            copy.start()

    def feed_chunk(turn, chunk):
        layer = 1 - turn
        base = 8 * turn + 2 * chunk
        h_copy(2 * turn + chunk).wait()
        if turn == 1:
            kin_right(True, 1, chunk).wait_send()
        slot = opened(base)

        def up_tile(here, index):
            there = pl.ds(pl.multiple_of(chunk * 1024 + index * 256, 256), 256)
            value = mm(pair[...], slots[slot, :, here]) * hbuf[:, here]
            short = value.astype(BF)
            slope[:, there] = short
            column = jnp.sum(short.astype(F32), axis=0, keepdims=True)
            for half in range(2):
                index_at = 7 + 4 * layer + 2 * half + chunk
                small_sum[0, index_at : index_at + 1, here] = jnp.where(
                    y_at == half, column, jnp.zeros_like(column)
                )

        tiles(4, up_tile)
        closed(base)
        if 2 * turn + chunk + 1 < 4:
            h_copy(2 * turn + chunk + 1).start(priority=LOCAL)
        kin_right(True, 2 * turn + 1, chunk).start()
        slot = opened(base + 1)

        def down_tile(there, _):
            value = mm_cols(slope[:, chunk * 1024 : chunk * 1024 + 1024], slots[slot, there, :])
            if chunk == 0:
                rows_sum[:, there] = value
            else:
                value = rows_sum[:, there] + value
                rows_sum[:, there] = value
                part_out[turn, :, there] = value[rows:].astype(BF)

        tiles(4, down_tile)
        closed(base + 1)
        if chunk == 1:
            if turn == 0:
                for copy in kin_lefts(True, 0):
                    copy.wait_send()
            part_over(turn).start()

    def row_steps(body, count):
        zero = jnp.zeros((1, width), F32)

        def step(index, carry):
            here = pl.ds(pl.multiple_of(index * 32, 32), 32)
            return tuple(a + b for a, b in zip(carry, body(here)))

        return lax.fori_loop(0, rows // 32, step, (zero,) * count)

    def lean(back, unit, inverse, gain):
        scaled = back * gain
        inner = (
            scaled
            - jnp.mean(scaled, axis=-1, keepdims=True)
            - unit * jnp.mean(scaled * unit, axis=-1, keepdims=True)
        )
        return inverse * inner, jnp.sum(back * unit, axis=0, keepdims=True)

    def feed_end(turn):
        layer = 1 - turn
        gain = gains[3 + layer : 4 + layer, :]
        part_over(turn).wait_recv()
        row_copy(2 * turn).wait()

        def body(here):
            unit, inverse = unit_rows(ub[here, :].astype(F32))
            back = rows_sum[here, :] + part_in[turn, here, :].astype(F32)
            dx, gain_part = lean(back, unit, inverse, gain)
            old = grad[here, :].astype(F32)
            grad[here, :] = (old + dx).astype(BF)
            return gain_part, jnp.sum(old, axis=0, keepdims=True)

        gain_grad, out_grad = row_steps(body, 2)
        row_copy(2 * turn + 1).start(priority=LOCAL)
        small_row(3 + layer, gain_grad)
        small_row(5 + layer, out_grad)
        grad_saved(turn).start(priority=LOCAL)
        slot = opened(8 * turn + 4)

        def tile(there, _):
            dob[:, there] = mm_cols(grad[...], slots[slot, there, :]).astype(BF)

        tiles(2, tile, 512)
        closed(8 * turn + 4)
        grad_saved(turn).wait()
        kin_right(False, 4 * turn, 0).start()

    def attend_heads(turn):
        scale = 1.0 / math.sqrt(HD)
        for copy in act_copies(turn):
            copy.wait()
        if turn == 1:
            for which in range(3):
                kin_right(False, 1 + which, 0).wait_send()

        def head(index, carry):
            here = pl.ds(pl.multiple_of(index * HD, HD), HD)
            q, k, v, do = qb[:, here], kb[:, here], vb[:, here], dob[:, here]
            scores = mm_cols(q, k) * scale
            if turn == 1:
                scores = jnp.where(mask_in[...] > 0.0, scores, MASKED)
            grown = jnp.exp(scores - jnp.max(scores, axis=-1, keepdims=True))
            soft = grown / jnp.sum(grown, axis=-1, keepdims=True)
            back = mm_cols(do, v)
            short = soft * (back - jnp.sum(soft * back, axis=-1, keepdims=True))
            dqkv[0, :, here] = (mm(short.astype(BF), k) * scale).astype(BF)
            dqkv[1, :, here] = (mm(short.T.astype(BF), q) * scale).astype(BF)
            dqkv[2, :, here] = mm(soft.T.astype(BF), do).astype(BF)
            return carry

        lax.fori_loop(0, width // HD, head, 0)
        if turn == 0:
            for copy in act_copies(1):
                copy.start(priority=LOCAL)
        for which in range(3):
            kin_right(False, 4 * turn + 1 + which, 0).start()

    def attend_end(turn):
        base = 8 * turn + 5
        for which in range(3):
            slot = opened(base + which)

            def tile(there, _):
                value = mm_cols(dqkv[which], slots[slot, there, :])
                if which == 0:
                    rows_sum[0:rows, there] = value
                elif which == 1:
                    rows_sum[rows : 2 * rows, there] = value
                else:
                    rows_sum[rows : 2 * rows, there] += value

            tiles(2, tile, 512)
            closed(base + which)
        row_copy(2 * turn + 1).wait()
        gain_q = gains[2:3, :] if turn == 0 else gains[0:1, :]
        gain_kv = gains[2:3, :] if turn == 0 else gains[1:2, :]

        def body(here):
            unit, inverse = unit_rows(ub[here, :].astype(F32))
            dx, gain_part = lean(rows_sum[here, :], unit, inverse, gain_q)
            if turn == 1:
                unit, inverse = unit_rows(src_in[here, :].astype(F32))
            there = pl.ds(pl.multiple_of(rows + here.start, 32), 32)
            ds, kv_part = lean(rows_sum[there, :], unit, inverse, gain_kv)
            fresh = grad[here, :].astype(F32) + dx
            if turn == 0:
                fresh += ds
            else:
                high = ds.astype(BF)
                part_out[0, here, :] = high
                part_out[1, here, :] = (ds - high.astype(F32)).astype(BF)
            grad[here, :] = fresh.astype(BF)
            return gain_part, kv_part

        if turn == 1:
            for which in range(2):
                part_over(which).wait_send()
            for copy in kin_lefts(True, 2):
                copy.wait_send()
        gain_grad, kv_grad = row_steps(body, 2)
        if turn == 0:
            row_copy(2).start(priority=LOCAL)
            small_row(2, gain_grad + kv_grad)
            open_pair(1)
        else:
            small_row(0, gain_grad)
            small_row(1, kv_grad)
            small_row(15, jnp.zeros_like(gain_grad))

            def tile(there, _):
                pair[:, there] = (
                    mm(picks_in[...], part_out[0, :, there])
                    + mm(picks_in[...], part_out[1, :, there])
                ).astype(BF)

            tiles(4, tile)
            small_copy(0).start()
            for which in range(3):
                point_copy(which).start()
            lat_start(1)

    def point_total():
        for which in range(3):
            point_copy(which).wait_recv()
        gathered = pair[
            pl.ds(pl.multiple_of(section_at * quarter_rows, 128), quarter_rows)
        ].astype(F32)
        for which in range(3):
            gathered += point_in[which].astype(F32)
        point_sum[...] = gathered.astype(BF)
        point_local().start(priority=LOCAL)
        for which in range(3):
            point_deal(which).start()

    def small_step(phase):
        small_copy(phase).wait_recv()
        small_sum[phase + 1] = small_sum[phase] + small_in[phase]
        if phase < 2:
            small_copy(phase + 1).start()
        else:
            for step in range(3):
                small_copy(3 + step).start()

    def small_end():
        for step in range(3):
            small_copy(3 + step).wait_recv()
        small_out[...] = (small_sum[3] + small_in[4]) + (small_in[3] + small_in[5])

    def rows_end():
        lat_onward(1)
        point_total()

    begin = pltpu.make_async_copy(top_in, grad, act_sems.at[4])
    begin.start()
    for index in range(2):
        slot_copy(index).start(priority=LOCAL)
    h_copy(0).start(priority=LOCAL)
    row_copy(0).start(priority=LOCAL)
    for copy in act_copies(0):
        copy.start(priority=LOCAL)
    begin.wait()
    open_pair(0)
    for part in range(2):
        kin_right(True, 0, part).start()
    pair_ready(0)
    for copy in kin_lefts(True, 1):
        copy.start()
    for job in range(4):
        for copy in kin_lefts(False, job):
            copy.start()
    for part in range(2):
        kin_right(True, 2, part).start()
    for copy in kin_lefts(True, 3):
        copy.start()
    for job in range(4, 8):
        for copy in kin_lefts(False, job):
            copy.start()
    raw_start(0)
    load(0)
    chain = {
        0: [functools.partial(feed_chunk, 0, 0), functools.partial(lat_start, 0)],
        1: [functools.partial(feed_chunk, 0, 1)],
        2: [functools.partial(feed_end, 0), functools.partial(lat_onward, 0)],
        3: [functools.partial(attend_heads, 0)],
        4: [functools.partial(attend_end, 0)],
        5: [functools.partial(pair_ready, 1), functools.partial(feed_chunk, 1, 0)],
        6: [functools.partial(feed_chunk, 1, 1)],
        7: [functools.partial(feed_end, 1)],
        8: [functools.partial(attend_heads, 1)],
        9: [functools.partial(attend_end, 1)],
        11: [functools.partial(small_step, 0), rows_end],
        13: [functools.partial(small_step, 1)],
        15: [functools.partial(small_step, 2)],
        17: [small_end],
    }

    def moment_body(moment, carry):
        @pl.when(moment < total)
        def _():
            by_kind(moment, offer)

        for lag, action in ((2, first), (3, second), (4, third), (5, close), (6, finish)):
            pl.when(jnp.logical_and(moment >= lag, moment < total + lag))(
                functools.partial(action, moment - lag)
            )
        for when, actions in chain.items():

            @pl.when(moment == when)
            def _():
                for action in actions:
                    action()

        for item in range(1, total):
            pl.when(moment == item - 1)(functools.partial(load, item))
        return carry

    lax.fori_loop(0, total + 6, moment_body, 0)

    for index in range(4):
        if index % 2 == 1:
            for copy in kin_lefts(True, index):
                copy.wait_send()
        if index != 1:
            for chunk in range(2):
                kin_right(True, index, chunk).wait_send()
    for index in range(8):
        for copy in kin_lefts(False, index):
            copy.wait_send()
        if index not in (1, 2, 3):
            kin_right(False, index, 0).wait_send()
    for phase in range(6):
        small_copy(phase).wait_send()
    for which in range(2):
        lat_local(which).wait()
        for way in range(2):
            lat_copy(which, way).wait_send()
            lat_far(which, way).wait()
    point_local().wait()
    for which in range(3):
        point_copy(which).wait_send()
        point_deal(which).wait()

    def drain(item, carry):
        @pl.when(item >= 4)
        def _():
            by_kind(item, drained)

        return carry

    for item in range(total - STAGES, total):
        xy_sent(item)
    lax.fori_loop(0, total, drain, 0)


def reduce_all(full, kept, latents, gains, mask, picks):
    total = ITEM_COUNT
    rows, width = kept[0].shape
    points = picks.shape[0]
    anywhere = pl.BlockSpec(memory_space=pl.ANY)
    vmem = pl.BlockSpec(memory_space=pltpu.VMEM)
    u1, u2, u3, u4, top = kept[:5]
    operands = [*full, u1, u2, u3, u4, top, *kept[5:16], *kept[17:], latents, kept[16]]
    operands += [gains, mask, picks]
    spaces = [anywhere] * (len(operands) - 4) + [vmem] * 4
    dma = pltpu.SemaphoreType.DMA
    flops = 2 * width * width * 24 * rows * 2
    return pl.pallas_call(
        reduce_kernel,
        out_shape=[
            jax.ShapeDtypeStruct((2, 128, 4 * width), BF),
            jax.ShapeDtypeStruct((2, 128, 4 * width), BF),
            jax.ShapeDtypeStruct((128, 3 * width), BF),
            jax.ShapeDtypeStruct((128, 3 * width), BF),
            jax.ShapeDtypeStruct((128, width), BF),
            jax.ShapeDtypeStruct((128, width), BF),
            jax.ShapeDtypeStruct((4 * rows, width), BF),
            jax.ShapeDtypeStruct((4 * rows, width), BF),
            jax.ShapeDtypeStruct((points, width), BF),
            jax.ShapeDtypeStruct((16, width), F32),
            jax.ShapeDtypeStruct((2, rows, width), BF),
            jax.ShapeDtypeStruct((4, 4, 2 * rows, 128), BF),
            jax.ShapeDtypeStruct((8, 4, rows, 128), BF),
            jax.ShapeDtypeStruct((4, 2 * rows, 2 * width), BF),
            jax.ShapeDtypeStruct((8, rows, width), BF),
        ],
        in_specs=spaces,
        out_specs=[anywhere] * 9 + [vmem] + [anywhere] * 5,
        scratch_shapes=[
            pltpu.VMEM((4, 4, 128, 1024), BF),
            pltpu.VMEM((8, 4, 128, 512), BF),
            pltpu.VMEM((4, 2, 512, 128), BF),
            pltpu.VMEM((WINDOWS, 1024, 1024), BF),
            pltpu.VMEM((STAGES, 4, 128, 512), BF),
            pltpu.VMEM((4, 4, 128, 1024), BF),
            pltpu.VMEM((8, 4, 128, 512), BF),
            pltpu.VMEM((8, 5, 128, 1024), BF),
            pltpu.VMEM((4, 128, 1024), BF),
            pltpu.VMEM((8, 128, 512), BF),
            pltpu.VMEM((4, 128, 1024), BF),
            pltpu.VMEM((8, 128, 512), BF),
            pltpu.VMEM((512, 1024), BF),
            pltpu.VMEM((512, 2048), BF),
            pltpu.VMEM((512, 1024), F32),
            pltpu.VMEM((512, 1024), F32),
            pltpu.VMEM((2, 1024, 1024), BF),
            pltpu.VMEM((256, 1024), BF),
            pltpu.VMEM((256, 1024), BF),
            pltpu.VMEM((256, 1024), BF),
            pltpu.VMEM((256, 1024), BF),
            pltpu.VMEM((3, 256, 1024), BF),
            pltpu.VMEM((2, 256, 1024), BF),
            pltpu.VMEM((2, 256, 1024), BF),
            pltpu.VMEM((256, 1024), BF),
            pltpu.VMEM((256, 1024), BF),
            pltpu.VMEM((3, points // 4, width), BF),
            pltpu.VMEM((points // 4, width), BF),
            pltpu.VMEM((6, 16, width), F32),
            pltpu.VMEM((4, 16, width), F32),
            dma((2, 12, 4)),
            dma((2, 16)),
            dma((4, 2)),
            dma((WINDOWS, 2)),
            dma((2, 8, 2)),
            dma((total, 4)),
            dma((total, 5)),
            dma((2, total, 2)),
            dma((2, total, 2)),
            dma((total, 2)),
            dma((2, 2, 2)),
            dma((2, 2, 2)),
            dma((2,)),
            dma((2, 3)),
            dma((2, 3)),
            dma((1,)),
            dma((2, 6)),
            dma((2, 2, 2)),
            dma((2,)),
            dma((1,)),
            dma((1,)),
            dma((5,)),
        ],
        compiler_params=pltpu.CompilerParams(
            collective_id=2, has_side_effects=True, vmem_limit_bytes=62 * 2**20
        ),
        cost_estimate=pl.CostEstimate(
            flops=flops, bytes_accessed=2**27, transcendentals=2**21
        ),
    )(*operands)[:10]


def plain_layers(full, spread, mine, source, valid, cot_own, picks, groups_all):
    proj_c, out_c, in_0, down_0, proj_s, out_s, in_1, down_1 = full
    width, hidden = in_0.shape

    def vector(first, count):
        return spread[:, first : first + count].reshape(-1)

    gains_cross = (vector(0, 1), vector(1, 1))
    gain_self = vector(2, 1)
    gains_mlp = (vector(3, 1), vector(4, 1))
    biases_out = (vector(5, 1), vector(6, 1))
    per_bias = hidden // width
    biases_in = (vector(7, per_bias), vector(7 + per_bias, per_bias))
    cot = cot_own.astype(F32)
    u1, kept_c = attend(mine, source, valid, gains_cross[0], gains_cross[1], proj_c, out_c)
    u2, kept_0 = feed(u1.astype(F32), gains_mlp[0], in_0, biases_in[0], down_0, biases_out[0])
    u2 = u2.astype(F32)
    u3, kept_s = attend(u2, u2, None, gain_self, gain_self, proj_s, out_s)
    u4, kept_1 = feed(u3.astype(F32), gains_mlp[1], in_1, biases_in[1], down_1, biases_out[1])
    final = u4.astype(F32)
    group_norm = jnp.sqrt(jnp.mean(final * final) + EPSILON)
    norm_mean = lax.psum(group_norm, ALL) / groups_all
    g4 = (cot + (norm_mean / group_norm) * final).astype(BF)

    dx, gain_1_grad, bias_1_grad, ob_1_grad, pairs_1 = feed_back(
        g4, kept_1, gains_mlp[1], in_1, down_1
    )
    g3 = (g4.astype(F32) + dx).astype(BF)
    dx, ds, gq, gkv, pairs_s = attend_back(g3, kept_s, gain_self, gain_self, proj_s, out_s)
    gain_s_grad = gq + gkv
    g2 = (g3.astype(F32) + dx + ds).astype(BF)
    dx, gain_0_grad, bias_0_grad, ob_0_grad, pairs_0 = feed_back(
        g2, kept_0, gains_mlp[0], in_0, down_0
    )
    g1 = (g2.astype(F32) + dx).astype(BF)
    dx, ds, cq_grad, ckv_grad, pairs_c = attend_back(
        g1, kept_c, gains_cross[0], gains_cross[1], proj_c, out_c
    )
    g0 = (g1.astype(F32) + dx).astype(BF)
    high = ds.astype(BF)
    low = (ds - high.astype(F32)).astype(BF)
    point_part = (mm_rows(picks, high) + mm_rows(picks, low)).astype(BF)
    small = jnp.concatenate(
        [
            cq_grad,
            ckv_grad,
            gain_s_grad,
            gain_0_grad,
            gain_1_grad,
            ob_0_grad,
            ob_1_grad,
            bias_0_grad,
            bias_1_grad,
            jnp.zeros_like(cq_grad),
        ]
    ).reshape(-1, width)
    pairs = pairs_1 + pairs_s + pairs_0 + pairs_c
    lefts, rights = [pair[0] for pair in pairs], [pair[1] for pair in pairs]
    def settled_grad(left, right):
        part = lax.psum_scatter(
            mm_rows(left, right).astype(BF), ALL, scatter_dimension=0, tiled=True
        )
        return lax.all_gather(part, "section", axis=0, tiled=True).astype(F32)

    done = [settled_grad(left, right) for left, right in pairs]
    mlp_in_grad = jnp.stack([done[6], done[0]])
    mlp_down_grad = jnp.stack([done[7], done[1]])
    proj_s_grad = jnp.concatenate(done[2:5], axis=1)
    proj_c_grad = jnp.concatenate(done[8:11], axis=1)
    out_s_grad, out_c_grad = done[5], done[11]
    points_sum = lax.psum(point_part, "section")
    latents_out = lax.all_gather(u4, "section", axis=0, tiled=True)
    g0_all = lax.all_gather(g0, "section", axis=0, tiled=True)
    small = lax.psum(small, ALL)
    return (
        norm_mean,
        latents_out,
        g0_all,
        points_sum,
        small,
        mlp_in_grad,
        mlp_down_grad,
        proj_c_grad,
        proj_s_grad,
        out_c_grad,
        out_s_grad,
    )


def per_device(
    latents,
    points,
    neighbours,
    lengths,
    cross_proj,
    cross_out,
    cross_gains,
    self_proj,
    self_out,
    self_gain,
    mlp_gain,
    mlp_in,
    mlp_in_bias,
    mlp_down,
    mlp_out_bias,
    cotangent,
):
    sections = lax.axis_size("section")
    section_at = lax.axis_index("section")
    width = latents.shape[1]
    hidden = mlp_in.shape[2]
    groups_dev = neighbours.shape[0]
    rows = latents.shape[0] // sections
    shard = cross_out.shape[0]
    piece = shard // sections
    groups_all = groups_dev * lax.axis_size("batch")

    def gathered(block):
        own = lax.dynamic_slice_in_dim(block, section_at * piece, piece, 0)
        return lax.all_gather(own, ALL, axis=0, tiled=True)

    projs = (cross_proj.reshape(shard, 3 * width), self_proj.reshape(shard, 3 * width))
    if lax.axis_size("batch") == 8:
        made = gather_forward(
            [projs[0], cross_out, mlp_in, mlp_down, projs[1], self_out],
            latents,
            cotangent,
            points,
            neighbours,
            lengths[:, None],
            [cross_gains, self_gain[None, :], mlp_gain, mlp_out_bias, mlp_in_bias],
        )
        full, gain_rows, norm_tile, mask, picks = made[:8], *made[8:12]
        norm_mean = norm_tile[0, 0]
        (
            mlp_in_grad,
            mlp_down_grad,
            proj_c_grad,
            proj_s_grad,
            out_c_grad,
            out_s_grad,
            latents_out,
            g0_all,
            points_sum,
            small,
        ) = reduce_all(full, made[12:], latents, gain_rows, mask, picks)
        mlp_in_grad = mlp_in_grad.astype(F32)
        mlp_down_grad = mlp_down_grad.astype(F32)
        proj_c_grad, proj_s_grad = proj_c_grad.astype(F32), proj_s_grad.astype(F32)
        out_c_grad, out_s_grad = out_c_grad.astype(F32), out_s_grad.astype(F32)
    else:
        vectors = jnp.concatenate(
            [
                cross_gains.reshape(-1),
                self_gain,
                mlp_gain.reshape(-1),
                mlp_out_bias.reshape(-1),
                mlp_in_bias.reshape(-1),
                jnp.zeros_like(self_gain),
            ]
        ).reshape(-1, shard)
        cot_own = lax.dynamic_slice_in_dim(cotangent, section_at * rows, rows, 0)
        mine = lax.dynamic_slice_in_dim(latents, section_at * rows, rows, 0).astype(F32)
        listed = lax.dynamic_index_in_dim(neighbours, section_at, 0, keepdims=False)
        length = lax.dynamic_index_in_dim(lengths, section_at, 0, keepdims=False)
        valid = jnp.arange(listed.shape[0], dtype=jnp.int32) < length
        picks = listed[:, None] == jnp.arange(points.shape[0], dtype=jnp.int32)[None, :]
        picks = picks.astype(BF)
        source = mm(picks, points)
        blocks = [projs[0], cross_out, mlp_in[0], mlp_down[0]]
        blocks += [projs[1], self_out, mlp_in[1], mlp_down[1]]
        full = [gathered(block) for block in blocks]
        spread = lax.all_gather(vectors, "batch", axis=0, tiled=False)
        (
            norm_mean,
            latents_out,
            g0_all,
            points_sum,
            small,
            mlp_in_grad,
            mlp_down_grad,
            proj_c_grad,
            proj_s_grad,
            out_c_grad,
            out_s_grad,
        ) = plain_layers(full, spread.astype(F32), mine, source, valid, cot_own, picks, groups_all)
    points_grad = points_sum.astype(F32)
    latents_grad = g0_all.astype(F32)
    per_bias = hidden // width
    batch_at = lax.axis_index("batch")

    def own(first, count):
        flat = small[first : first + count].reshape(-1)
        size = flat.shape[0] // lax.axis_size("batch")
        return lax.dynamic_slice_in_dim(flat, batch_at * size, size, 0)

    return (
        latents_out,
        latents_grad,
        points_grad,
        proj_c_grad.reshape(shard, 3, width),
        out_c_grad,
        jnp.stack([own(0, 1), own(1, 1)]),
        proj_s_grad.reshape(shard, 3, width),
        out_s_grad,
        own(2, 1),
        jnp.stack([own(3, 1), own(4, 1)]),
        mlp_in_grad,
        jnp.stack([own(7, per_bias), own(7 + per_bias, per_bias)]),
        mlp_down_grad,
        jnp.stack([own(5, 1), own(6, 1)]),
        norm_mean,
    )


def solution(mesh):
    rows = P("batch", None)
    cols = P(None, "batch")
    block = P("batch", None, None)
    pair = P(None, "batch", None)
    return jax.shard_map(
        per_device,
        mesh=mesh,
        in_specs=(
            rows,
            rows,
            rows,
            P("batch"),
            block,
            rows,
            cols,
            block,
            rows,
            P("batch"),
            cols,
            pair,
            cols,
            pair,
            cols,
            rows,
        ),
        out_specs=(
            rows,
            rows,
            rows,
            block,
            rows,
            cols,
            block,
            rows,
            P("batch"),
            cols,
            pair,
            cols,
            pair,
            cols,
            P(),
        ),
        check_vma=False,
    )
```

profile of v0, /device:TPU:0, one launch (start us, length us, event | category | flops | bytes accessed | tf_op | source)
XLA Modules:
  0.0 502.8 jit_solution(1239902245398388568)
XLA Ops:
  0.7 1.4 copy.40.refs_10_
  2.0 1.5 copy.36
  3.6 1.2 copy.38.refs_0_
  5.1 1.2 copy.39.refs_4_
  6.3 197.3 %shard_map.271 = (bf16[1024,3072]{1,0:T(8,128)(2,1)}, bf16[1024,1024]{1,0:T(8,128)(2,1)}, bf16[1024,2048]{1,0:T(8,128)(2,1)}, bf16[1024,2048]{1,0:T(8,128)(2,1)}...) custom-call(bf16[128,3072]{1,0:T(8,128)(2,1)} %copy.38.refs_0_, ...), custom_call_target="tpu_custom_call" | custom-call | flops 8589934592 | bytes 134217728 | tf_op jit(solution)/shard_map/pallas_call | solution.py:736
  203.6 1.2 slice.39
  204.8 274.1 %shard_map.272 = (bf16[2,128,4096]{2,1,0:T(8,128)(2,1)}, bf16[2,128,4096]{2,1,0:T(8,128)(2,1)}, bf16[128,3072]{1,0:T(8,128)(2,1)}, bf16[128,3072]{1,0:T(8,128)(2...) custom-call(bf16[1024,3072]{1,0:T(8,128)(2,1)} %get-tuple-element.57, ...), custom_call_target="tpu_custom_call" | custom-call | flops 25769803776 | bytes 134217728 | tf_op jit(solution)/shard_map/pallas_call | solution.py:1812
  478.9 1.0 fusion.1
  480.0 0.9 slice_bitcast_fusion.1
  480.8 0.6 pad_maximum_fusion.3
  481.5 0.6 pad_maximum_fusion
  482.2 0.5 fusion
  482.7 0.6 pad_maximum_fusion.1
  483.2 0.6 pad_maximum_fusion.2
  483.8 1.8 convert_element_type.22
  485.6 1.8 convert_element_type.23
  487.7 1.6 copy.43
  489.6 1.6 copy.44
  491.2 1.6 convert_element_type.21
  492.8 0.8 copy-done.2
  493.6 2.5 convert_element_type.20
  496.0 2.5 convert_element_type.24
  498.5 2.5 convert_element_type.25
  501.0 1.3 copy.50
  (24 shorter events, 1.1 us)
Async XLA Ops:
  0.6 4.1 copy-start.5
  478.9 8.5 %copy-start.7 = (bf16[128,3072]{1,0:T(8,128)(2,1)S(1)}, bf16[128,3072]{1,0:T(8,128)(2,1)}, u32[]{:S(2)}) copy-start(bf16[128,3072]{1,0:T(8,128)(2,1)} %get-tuple-element.91) | copy-start | bytes 2359300
  487.7 1.6 copy-start.6
  489.6 1.6 copy-start.4
  491.2 2.3 copy-start.2
  493.5 2.5 copy-start.1
  496.0 2.5 copy-start
  498.5 2.5 copy-start.3
where the time goes:
time: 512 us; the launch traced here: 503 us
  Pallas kernels  471 us (92%)
  local copies, waits for them, and re-layouts  15.2 us (3%)
  other arithmetic  14.9 us (3%)
    pallas_call x1, Pallas kernels, reduce_all(): pl.pallas_call(reduce_kernel, out_shape=[jax.ShapeDtypeStruct((2, 128, 4...  274 us
    pallas_call x1, Pallas kernels, gather_forward(): pl.pallas_call(gather_kernel, out_shape=[jax.ShapeDtypeStruct((width, siz...  197 us

commit v1 on v0

--- a/solution.py
+++ b/solution.py
@@ -782,6 +782,8 @@
 
 
 ITEM_COUNT = 16
+FEEDS = (0, 1, 2, 4, 6, 9, 10, 13)
+ATTENDS = (3, 5, 7, 8, 11, 12, 14, 15)
 WINDOWS = 4
 STAGES = 3
 
@@ -833,7 +835,8 @@
         stage,
         merged_f,
         merged_a,
-        passing,
+        passing_f,
+        passing_a,
         lined_f,
         lined_a,
         crossed_f,
@@ -856,7 +859,7 @@
         point_sum,
         small_in,
         small_sum,
-    ) = refs[47:77]
+    ) = refs[47:78]
     (
         kin_l_sems,
         kin_r_sems,
@@ -880,7 +883,7 @@
         h_sem,
         save_sems,
         act_sems,
-    ) = refs[77:]
+    ) = refs[78:]
     section_at = lax.axis_index("section")
     batch_at = lax.axis_index("batch")
     core = lax.rem(batch_at, 2)
@@ -947,10 +950,10 @@
         return remote(source, target, kin_r_sems, where, (section_at, sibling))
 
     def item_of(index):
-        turn, inner = index // 8, index % 8
-        if inner < 4:
-            return True, 2 * turn + inner // 2, inner % 2
-        return False, 4 * turn + inner - 4, 0
+        if index in FEEDS:
+            order = FEEDS.index(index)
+            return True, order // 2, order % 2
+        return False, ATTENDS.index(index), 0
 
     def window_copies(index):
         feed, job, chunk = item_of(index)
@@ -998,6 +1001,8 @@
         for copy in window_copies(index):
             copy.start(priority=LOCAL)
         if chunk == 0:
+            if feed and job == 2:
+                raw_start(index)
             size = 512 if feed else 256
             target = (lwin_f if feed else lwin_a).at[job]
             for part in range(4):
@@ -1005,17 +1010,14 @@
                     copy.wait()
                     place = raw.at[part, whose, pl.ds(0, size)]
                     target[part, :, whose * size : whose * size + size] = place[...].T
-        if index + 1 < total:
+        if index + 1 < total and item_of(index + 1)[:2] != (True, 2):
             raw_start(index + 1)
 
+    def count_below(item, places):
+        return sum((item > place).astype(jnp.int32) for place in places)
+
     def is_feed(item):
-        return lax.rem(item, 8) < 4
-
-    def feed_job(item):
-        return 2 * (item // 8) + lax.rem(item, 8) // 2
-
-    def att_job(item):
-        return 4 * (item // 8) + lax.rem(item, 8) - 4
+        return functools.reduce(jnp.logical_or, [item == place for place in FEEDS])
 
     def loaded(slot, feed):
         size = 512 if feed else 256
@@ -1026,30 +1028,37 @@
             ).wait()
 
     def by_kind(item, action):
-        pl.when(is_feed(item))(functools.partial(action, item, True))
-        pl.when(jnp.logical_not(is_feed(item)))(functools.partial(action, item, False))
-
-    def merged_of(item, feed):
-        return merged_f.at[lax.rem(item, 4)] if feed else merged_a.at[att_job(item)]
-
-    def passing_of(item, feed, slot):
-        ref = passing.at[lax.rem(item, 8), slot]
-        return ref if feed else ref.at[:, pl.ds(0, 512)]
-
-    def lined_of(item, feed):
-        return lined_f.at[lax.rem(item, 4)] if feed else lined_a.at[att_job(item)]
-
-    def crossed_of(item, feed):
-        return crossed_f.at[lax.rem(item, 4)] if feed else crossed_a.at[att_job(item)]
-
-    def products(item, choice, store):
-        slot = lax.rem(item, WINDOWS)
-
+        @pl.when(is_feed(item))
+        def _():
+            action(count_below(item, FEEDS), True)
+
+        @pl.when(jnp.logical_not(is_feed(item)))
+        def _():
+            action(count_below(item, ATTENDS), False)
+
+    def mark(order, feed):
+        return order if feed else 8 + order
+
+    def merged_of(order, feed):
+        return merged_f.at[lax.rem(order, 4)] if feed else merged_a.at[order]
+
+    def passing_of(order, feed, slot):
+        if feed:
+            return passing_f.at[lax.rem(order, 6), slot]
+        return passing_a.at[lax.rem(order, 4), slot]
+
+    def lined_of(order, feed):
+        return lined_f.at[lax.rem(order, 4)] if feed else lined_a.at[order]
+
+    def crossed_of(order, feed):
+        return crossed_f.at[lax.rem(order, 4)] if feed else crossed_a.at[order]
+
+    def products(order, slot, choice, store):
         def quarter(index, carry):
             here = pl.ds(pl.multiple_of(index * 256, 256), 256)
             bit = choice[0] + index * (choice[1] - choice[0])
             first = pl.multiple_of(index * 512 + bit * 256, 256)
-            left = lwin_a[att_job(item)].reshape(512, 512)
+            left = lwin_a[order].reshape(512, 512)
             right = rwin[slot, 0:512, pl.ds(first, 256)]
             tile = jnp.dot(left, right, preferred_element_type=F32).reshape(4, 128, 256)
             store(pl.ds(0, 4), here, tile)
@@ -1060,10 +1069,10 @@
     def xy_copies(item):
         return [
             remote(
-                stage.at[lax.rem(att_job(item), STAGES), :, :, pl.ds(side * 256, 256)],
-                merged_a.at[att_job(item), :, :, pl.ds(side * 256, 256)],
+                stage.at[lax.rem(item, STAGES), :, :, pl.ds(side * 256, 256)],
+                merged_a.at[item, :, :, pl.ds(side * 256, 256)],
                 xy_sems,
-                (att_job(item), side),
+                (item, side),
                 (flat[side], batch_at),
             )
             for side in range(2)
@@ -1079,8 +1088,8 @@
         return pltpu.make_async_remote_copy(
             merged_of(item, feed).at[dest],
             passing_of(item, feed, slot),
-            line_send.at[item, dest],
-            line_recv.at[item, slot],
+            line_send.at[mark(item, feed), dest],
+            line_recv.at[mark(item, feed), slot],
             device_id=(section_at, batch_at + 2 * step),
             device_id_type=MESH,
         )
@@ -1089,8 +1098,8 @@
         pltpu.make_async_remote_copy(
             merged_of(item, feed).at[0],
             passing_of(item, feed, slot),
-            line_send.at[item, 0],
-            line_recv.at[item, slot],
+            line_send.at[mark(item, feed), 0],
+            line_recv.at[mark(item, feed), slot],
             device_id=(section_at, sibling),
             device_id_type=MESH,
         ).wait_recv()
@@ -1101,8 +1110,8 @@
             pltpu.make_async_remote_copy(
                 merged_of(item, feed).at[dest],
                 passing_of(item, feed, 0),
-                line_send.at[item, dest],
-                line_recv.at[item, 0],
+                line_send.at[mark(item, feed), dest],
+                line_recv.at[mark(item, feed), 0],
                 device_id=(section_at, sibling),
                 device_id_type=MESH,
             ).wait_send()
@@ -1120,6 +1129,9 @@
 
     def drained(item, feed):
         line_sent(item, feed)
+        delivered(item, feed)
+
+    def delivered(item, feed):
         if feed:
             feed_out(item, up_out).wait()
             feed_own(item, up_out).wait()
@@ -1128,20 +1140,19 @@
                 att_out(item, side, end_out_s, 0).wait()
                 att_own(item, side, end_out_s, 0).wait()
 
-    def offer(item, feed):
-        slot = lax.rem(item, WINDOWS)
+    def offer(slot, item, feed):
         loaded(slot, feed)
         if feed:
 
-            @pl.when(item >= 8)
+            @pl.when(item >= 4)
             def _():
-                drained(item - 8, True)
+                line_sent(item - 4, True)
 
             target = merged_of(item, True)
 
             def tile(index, carry):
                 here = pl.ds(pl.multiple_of(index * 256, 256), 256)
-                left = lwin_f[feed_job(item)].reshape(512, 1024)
+                left = lwin_f[item // 2].reshape(512, 1024)
                 right = rwin[slot, :, here]
                 value = jnp.dot(left, right, preferred_element_type=F32)
                 target[:, :, here] = value.reshape(4, 128, 256).astype(BF)
@@ -1151,34 +1162,27 @@
             outset(item, True)
         else:
 
-            @pl.when(lax.rem(item, 8) >= 4 + STAGES)
+            @pl.when(item >= STAGES)
             def _():
                 xy_sent(item - STAGES)
 
-            @pl.when(jnp.logical_and(item >= 12, lax.rem(item, 8) < 4 + STAGES))
-            def _():
-                xy_sent(item - STAGES - 4)
-
             def store(blocks, here, tile):
-                stage[lax.rem(att_job(item), STAGES), blocks, :, here] = tile.astype(BF)
-
-            products(item, (1 - x_at, 1 - y_at), store)
+                stage[lax.rem(item, STAGES), blocks, :, here] = tile.astype(BF)
+
+            products(item, slot, (1 - x_at, 1 - y_at), store)
             for copy in xy_copies(item):
                 copy.start()
 
-    def take(item):
+    def take(slot, item, feed):
         for copy in xy_copies(item):
             copy.wait_recv()
-        target = merged_a.at[att_job(item)]
+        target = merged_a.at[item]
 
         def store(blocks, here, tile):
             target[blocks, :, here] = (tile + target[blocks, :, here].astype(F32)).astype(BF)
 
-        products(item, bits, store)
+        products(item, slot, bits, store)
         outset(item, False)
-
-    def first(item):
-        pl.when(jnp.logical_not(is_feed(item)))(functools.partial(take, item))
 
     def relay(item, feed, dest, place, rightward):
         line_wait(item, feed, dest)
@@ -1206,12 +1210,6 @@
         @pl.when(spot == 2)
         def _():
             relay(item, feed, 3, 2, True)
-
-    def second(item):
-        by_kind(item, second_of)
-
-    def third(item):
-        by_kind(item, third_of)
 
     def feed_cross(item):
         return remote(
@@ -1228,16 +1226,13 @@
             lined_of(item, False).at[:, here],
             crossed_of(item, False).at[:, here],
             cross_sems,
-            (item, side),
+            (8 + item, side),
             (flat[1 - side], batch_at),
         )
-
-    def layer_of(item):
-        return 1 - item // 8
 
     def feed_place(item, target):
         base = y_at * 2048 + lax.rem(item, 2) * 1024
-        return target.at[layer_of(item), :, pl.ds(pl.multiple_of(base, 1024), 1024)]
+        return target.at[1 - item // 4, :, pl.ds(pl.multiple_of(base, 1024), 1024)]
 
     def feed_out(item, target):
         return remote(
@@ -1254,26 +1249,26 @@
         )
 
     def feed_write(item):
-        @pl.when(lax.rem(item, 8) < 2)
+        @pl.when(lax.rem(item, 4) < 2)
         def _():
             feed_out(item, down_out).start()
             feed_own(item, down_out).start(priority=LOCAL)
 
-        @pl.when(lax.rem(item, 8) >= 2)
+        @pl.when(lax.rem(item, 4) >= 2)
         def _():
             feed_out(item, up_out).start()
             feed_own(item, up_out).start(priority=LOCAL)
 
     def att_place(item, side, target, inner):
-        base = inner * 1024 + side * 512 + bits[side] * 256
-        return target.at[:, pl.ds(pl.multiple_of(base, 256), 256)]
+        base = side * 512 + bits[side] * 256
+        return target.at[inner, :, pl.ds(pl.multiple_of(base, 256), 256)]
 
     def att_out(item, side, target, inner):
         return remote(
             lined_of(item, False).at[:, pl.ds(side * 256, 256)],
             att_place(item, side, target, inner),
             out_sems,
-            (item, side),
+            (8 + item, side),
             (flat[side], batch_at),
         )
 
@@ -1281,26 +1276,32 @@
         return pltpu.make_async_copy(
             lined_of(item, False).at[:, pl.ds(side * 256, 256)],
             att_place(item, side, target, inner),
-            own_sems.at[item, side],
+            own_sems.at[8 + item, side],
         )
 
     def att_write(item):
-        inner = lax.rem(item, 8) - 5
+        inner = lax.rem(item, 4) - 1
         for turn, proj, end in ((0, proj_out_s, end_out_s), (1, proj_out_c, end_out_c)):
 
-            @pl.when(jnp.logical_and(item // 8 == turn, inner >= 0))
+            @pl.when(jnp.logical_and(item // 4 == turn, inner >= 0))
             def _():
                 for side in range(2):
                     att_out(item, side, proj, inner).start()
                     att_own(item, side, proj, inner).start(priority=LOCAL)
 
-            @pl.when(jnp.logical_and(item // 8 == turn, inner < 0))
+            @pl.when(jnp.logical_and(item // 4 == turn, inner < 0))
             def _():
                 for side in range(2):
                     att_out(item, side, end, 0).start()
                     att_own(item, side, end, 0).start(priority=LOCAL)
 
     def close_of(item, feed):
+        if feed:
+
+            @pl.when(item >= 4)
+            def _():
+                delivered(item - 4, True)
+
         for place in range(4):
 
             @pl.when(spot == place)
@@ -1319,9 +1320,6 @@
         else:
             for side in range(2):
                 cross_copy(item, side).start()
-
-    def close(item):
-        by_kind(item, close_of)
 
     def finish_of(item, feed):
         if feed:
@@ -1337,9 +1335,6 @@
             feed_write(item)
         else:
             att_write(item)
-
-    def finish(item):
-        by_kind(item, finish_of)
 
     def small_copy(phase):
         if phase == 0:
@@ -1742,12 +1737,19 @@
     def moment_body(moment, carry):
         @pl.when(moment < total)
         def _():
-            by_kind(moment, offer)
-
-        for lag, action in ((2, first), (3, second), (4, third), (5, close), (6, finish)):
-            pl.when(jnp.logical_and(moment >= lag, moment < total + lag))(
-                functools.partial(action, moment - lag)
-            )
+            by_kind(moment, functools.partial(offer, lax.rem(moment, WINDOWS)))
+
+        ready = jnp.logical_and(moment >= 2, moment < total + 2)
+
+        @pl.when(jnp.logical_and(ready, jnp.logical_not(is_feed(moment - 2))))
+        def _():
+            take(lax.rem(moment - 2, WINDOWS), count_below(moment - 2, ATTENDS), False)
+
+        for lag, action in ((3, second_of), (4, third_of), (5, close_of), (6, finish_of)):
+
+            @pl.when(jnp.logical_and(moment >= lag, moment < total + lag))
+            def _():
+                by_kind(moment - lag, action)
         for when, actions in chain.items():
 
             @pl.when(moment == when)
@@ -1785,16 +1787,17 @@
         point_copy(which).wait_send()
         point_deal(which).wait()
 
-    def drain(item, carry):
-        @pl.when(item >= 4)
+    def drain(order, carry):
+        @pl.when(order >= 4)
         def _():
-            by_kind(item, drained)
-
+            drained(order, True)
+
+        drained(order, False)
         return carry
 
-    for item in range(total - STAGES, total):
-        xy_sent(item)
-    lax.fori_loop(0, total, drain, 0)
+    for order in (5, 6, 7):
+        xy_sent(order)
+    lax.fori_loop(0, 8, drain, 0)
 
 
 def reduce_all(full, kept, latents, gains, mask, picks):
@@ -1814,10 +1817,10 @@
         out_shape=[
             jax.ShapeDtypeStruct((2, 128, 4 * width), BF),
             jax.ShapeDtypeStruct((2, 128, 4 * width), BF),
-            jax.ShapeDtypeStruct((128, 3 * width), BF),
-            jax.ShapeDtypeStruct((128, 3 * width), BF),
-            jax.ShapeDtypeStruct((128, width), BF),
-            jax.ShapeDtypeStruct((128, width), BF),
+            jax.ShapeDtypeStruct((3, 128, width), BF),
+            jax.ShapeDtypeStruct((3, 128, width), BF),
+            jax.ShapeDtypeStruct((1, 128, width), BF),
+            jax.ShapeDtypeStruct((1, 128, width), BF),
             jax.ShapeDtypeStruct((4 * rows, width), BF),
             jax.ShapeDtypeStruct((4 * rows, width), BF),
             jax.ShapeDtypeStruct((points, width), BF),
@@ -1838,7 +1841,8 @@
             pltpu.VMEM((STAGES, 4, 128, 512), BF),
             pltpu.VMEM((4, 4, 128, 1024), BF),
             pltpu.VMEM((8, 4, 128, 512), BF),
-            pltpu.VMEM((8, 5, 128, 1024), BF),
+            pltpu.VMEM((6, 5, 128, 1024), BF),
+            pltpu.VMEM((4, 5, 128, 512), BF),
             pltpu.VMEM((4, 128, 1024), BF),
             pltpu.VMEM((8, 128, 512), BF),
             pltpu.VMEM((4, 128, 1024), BF),
@@ -2041,8 +2045,9 @@
         ) = reduce_all(full, made[12:], latents, gain_rows, mask, picks)
         mlp_in_grad = mlp_in_grad.astype(F32)
         mlp_down_grad = mlp_down_grad.astype(F32)
-        proj_c_grad, proj_s_grad = proj_c_grad.astype(F32), proj_s_grad.astype(F32)
-        out_c_grad, out_s_grad = out_c_grad.astype(F32), out_s_grad.astype(F32)
+        proj_c_grad = jnp.swapaxes(proj_c_grad, 0, 1).astype(F32)
+        proj_s_grad = jnp.swapaxes(proj_s_grad, 0, 1).astype(F32)
+        out_c_grad, out_s_grad = out_c_grad[0].astype(F32), out_s_grad[0].astype(F32)
     else:
         vectors = jnp.concatenate(
             [

time: 512 us -> 499 us (0.975)
  Pallas kernels: 471 us -> 462 us
    pallas_call x1, Pallas kernels: 274 us -> 264 us  [reduce_all(): pl.pallas_call(reduce_kernel, out_shape=[jax.ShapeDtypeStruct((2, 128, 4...]
where the time goes in v1:
time: 499 us; the launch traced here: 489 us
  Pallas kernels  462 us (93%)
  other arithmetic  15.6 us (3%)
  local copies, waits for them, and re-layouts  10.9 us (2%)
    pallas_call x1, Pallas kernels, reduce_all(): pl.pallas_call(reduce_kernel, out_shape=[jax.ShapeDtypeStruct((2, 128, 4...  264 us
    pallas_call x1, Pallas kernels, gather_forward(): pl.pallas_call(gather_kernel, out_shape=[jax.ShapeDtypeStruct((width, siz...  197 us

profile of v1, /device:TPU:0, one launch (start us, length us, event | category | flops | bytes accessed | tf_op | source)
XLA Modules:
  0.0 489.2 jit_solution(8928375866002974052)
XLA Ops:
  0.7 1.4 copy.38.refs_10_
  2.0 1.5 copy.34
  3.6 1.2 copy.36.refs_0_
  4.7 0.4 copy.35
  5.1 1.2 copy.37.refs_4_
  6.3 197.4 %shard_map.271 = (bf16[1024,3072]{1,0:T(8,128)(2,1)}, bf16[1024,1024]{1,0:T(8,128)(2,1)}, bf16[1024,2048]{1,0:T(8,128)(2,1)}, bf16[1024,2048]{1,0:T(8,128)(2,1)}...) custom-call(bf16[128,3072]{1,0:T(8,128)(2,1)} %copy.36.refs_0_, ...), custom_call_target="tpu_custom_call" | custom-call | flops 8589934592 | bytes 134217728 | tf_op jit(solution)/shard_map/pallas_call | solution.py:736
  203.7 1.2 slice.39
  204.9 264.3 %shard_map.272 = (bf16[2,128,4096]{2,1,0:T(8,128)(2,1)}, bf16[2,128,4096]{2,1,0:T(8,128)(2,1)}, bf16[3,128,1024]{2,1,0:T(8,128)(2,1)}, bf16[3,128,1024]{2,1,0:T(...) custom-call(bf16[1024,3072]{1,0:T(8,128)(2,1)} %get-tuple-element.57, ...), custom_call_target="tpu_custom_call" | custom-call | flops 25769803776 | bytes 134217728 | tf_op jit(solution)/shard_map/pallas_call | solution.py:1815
  469.2 1.2 fusion.1
  470.4 0.9 slice_bitcast_fusion.1
  471.2 0.6 pad_maximum_fusion.3
  471.9 0.1 dynamic_slice.35
  472.0 0.6 pad_maximum_fusion
  472.6 0.5 fusion
  473.1 0.6 pad_maximum_fusion.1
  473.7 0.6 pad_maximum_fusion.2
  474.2 2.2 bitcast_convert_fusion
  476.5 1.6 convert_element_type.37
  478.0 2.0 convert_bitcast_fusion
  480.1 0.1 copy-done.2
  480.2 2.5 convert_element_type.36
  482.7 2.5 convert_element_type.46
  485.2 2.5 convert_element_type.47
  487.7 1.3 copy.44
  (20 shorter events, 0.1 us)
Async XLA Ops:
  0.6 4.1 copy-start.7
  469.2 7.3 %copy-start.4 = (bf16[512,1024]{1,0:T(8,128)(2,1)S(1)}, bf16[512,1024]{1,0:T(8,128)(2,1)}, u32[]{:S(2)}) copy-start(bf16[512,1024]{1,0:T(8,128)(2,1)} %get-tuple-element.90) | copy-start | bytes 3145732
  474.2 3.8 copy-start.5
  474.2 3.8 copy-start.6
  478.0 2.2 copy-start.2
  480.2 2.5 copy-start.1
  482.7 2.5 copy-start
  485.2 2.5 copy-start.3

commit v2 on v1

--- a/solution.py
+++ b/solution.py
@@ -16,7 +16,7 @@
 ALL = ("batch", "section")
 MESH = pl.DeviceIdType.MESH
 GATHER_WIDTH = 1024
-AHEAD = 4
+AHEAD = 6
 LOCAL = 1
 SLOTS = 3
 GATHERED = tuple(
@@ -1718,10 +1718,10 @@
     raw_start(0)
     load(0)
     chain = {
-        0: [functools.partial(feed_chunk, 0, 0), functools.partial(lat_start, 0)],
-        1: [functools.partial(feed_chunk, 0, 1)],
-        2: [functools.partial(feed_end, 0), functools.partial(lat_onward, 0)],
-        3: [functools.partial(attend_heads, 0)],
+        0: [functools.partial(feed_chunk, 0, 0)],
+        1: [functools.partial(feed_chunk, 0, 1), functools.partial(lat_start, 0)],
+        2: [functools.partial(feed_end, 0)],
+        3: [functools.partial(attend_heads, 0), functools.partial(lat_onward, 0)],
         4: [functools.partial(attend_end, 0)],
         5: [functools.partial(pair_ready, 1), functools.partial(feed_chunk, 1, 0)],
         6: [functools.partial(feed_chunk, 1, 1)],

time: 499 us -> 501 us (level)
  no operation moved by 1% of the time
where the time goes in v2:
time: 501 us; the launch traced here: 492 us
  Pallas kernels  464 us (93%)
  other arithmetic  15.6 us (3%)
  local copies, waits for them, and re-layouts  10.9 us (2%)
    pallas_call x1, Pallas kernels, reduce_all(): pl.pallas_call(reduce_kernel, out_shape=[jax.ShapeDtypeStruct((2, 128, 4...  262 us
    pallas_call x1, Pallas kernels, gather_forward(): pl.pallas_call(gather_kernel, out_shape=[jax.ShapeDtypeStruct((width, siz...  202 us

profile of v2, /device:TPU:0, one launch (start us, length us, event | category | flops | bytes accessed | tf_op | source)
XLA Modules:
  0.0 491.6 jit_solution(11108670364355306885)
XLA Ops:
  0.7 1.4 copy.38.refs_10_
  2.0 1.5 copy.34
  3.6 1.2 copy.36.refs_0_
  4.7 0.4 copy.35
  5.1 1.2 copy.37.refs_4_
  6.3 201.6 %shard_map.271 = (bf16[1024,3072]{1,0:T(8,128)(2,1)}, bf16[1024,1024]{1,0:T(8,128)(2,1)}, bf16[1024,2048]{1,0:T(8,128)(2,1)}, bf16[1024,2048]{1,0:T(8,128)(2,1)}...) custom-call(bf16[128,3072]{1,0:T(8,128)(2,1)} %copy.36.refs_0_, ...), custom_call_target="tpu_custom_call" | custom-call | flops 8589934592 | bytes 134217728 | tf_op jit(solution)/shard_map/pallas_call | solution.py:736
  207.9 1.2 slice.39
  209.1 262.3 %shard_map.272 = (bf16[2,128,4096]{2,1,0:T(8,128)(2,1)}, bf16[2,128,4096]{2,1,0:T(8,128)(2,1)}, bf16[3,128,1024]{2,1,0:T(8,128)(2,1)}, bf16[3,128,1024]{2,1,0:T(...) custom-call(bf16[1024,3072]{1,0:T(8,128)(2,1)} %get-tuple-element.57, ...), custom_call_target="tpu_custom_call" | custom-call | flops 25769803776 | bytes 134217728 | tf_op jit(solution)/shard_map/pallas_call | solution.py:1815
  471.3 1.2 fusion.1
  472.5 0.9 slice_bitcast_fusion.1
  473.4 0.6 pad_maximum_fusion.3
  474.0 0.1 dynamic_slice.36
  474.1 0.6 pad_maximum_fusion
  474.7 0.5 fusion
  475.2 0.6 pad_maximum_fusion.1
  475.8 0.6 pad_maximum_fusion.2
  476.4 2.2 bitcast_convert_fusion
  478.6 1.6 convert_element_type.37
  480.2 2.0 convert_bitcast_fusion
  482.2 0.1 copy-done.2
  482.3 2.5 convert_element_type.36
  484.8 2.5 convert_element_type.46
  487.3 2.5 convert_element_type.47
  489.8 1.3 copy.44
  (20 shorter events, 0.1 us)
Async XLA Ops:
  0.6 4.1 copy-start.7
  471.3 7.3 %copy-start.4 = (bf16[512,1024]{1,0:T(8,128)(2,1)S(1)}, bf16[512,1024]{1,0:T(8,128)(2,1)}, u32[]{:S(2)}) copy-start(bf16[512,1024]{1,0:T(8,128)(2,1)} %get-tuple-element.90) | copy-start | bytes 3145732
  476.4 3.8 copy-start.5
  476.4 3.8 copy-start.6
  480.2 2.2 copy-start.2
  482.3 2.5 copy-start.1
  484.8 2.5 copy-start
  487.3 2.5 copy-start.3
